TPU v7x, 32 devices: a whole 2x2x4 slice. The times are simulated.
32 devices in a mesh: dp: 8 (over y, x, core), tensor: 4 (over z).
Axes of the slice: x: 2, y: 2, z: 4, core: 2. Of those that a mesh axis runs over, the one named last changes fastest.
Arguments:
- x_tokens: bfloat16 [512, 8192], P('dp', 'tensor'), may hold values from -6 to 6
- sign_bits: int32 [8192], P('tensor'), may hold values from 0 to 1
- weight: bfloat16 [8192, 28672], P('tensor', 'dp'), may hold values from -0.0625 to 0.0625
- upstream: bfloat16 [512, 28672], P('tensor', 'dp'), may hold values from -0.25 to 0.25
Outputs:
- projected: bfloat16 [512, 28672], P('tensor', 'dp')
- weight_grad: float32 [8192, 28672], P('tensor', 'dp')
All inputs are finite; a program needn't handle non-finite values.
Results may differ from a plain program's by a relative error of at most 0.028.
Values may be sent and summed in bfloat16 or wider, within the bound.
No kernel may reach another device: no remote copies, remote signals or barrier semaphores. Data moves between devices by JAX's collectives and lax.ppermute only.
A program may use at most 128 MiB of HBM per device.

v0:
```python
import functools
import math

import jax
import jax.numpy as jnp
from jax import lax
from jax.experimental import pallas as pl
from jax.experimental.pallas import tpu as pltpu
from jax.sharding import PartitionSpec as P

MIB = 1 << 20
VMEM = pl.BlockSpec(memory_space=pltpu.VMEM)


def hadamard(order):
    row_ids = jnp.arange(order, dtype=jnp.int32)[:, None]
    col_ids = jnp.arange(order, dtype=jnp.int32)[None, :]
    common = row_ids & col_ids
    parity = jnp.zeros((order, order), jnp.int32)
    for section_bit in range(max(order.bit_length() - 1, 0)):
        parity = parity + (common >> section_bit & 1)
    return (1 - 2 * (parity % 2)).astype(jnp.bfloat16)


def swap(block, axis, mask):
    count = lax.axis_size(axis)
    return lax.ppermute(
        block, axis, [(i, i ^ mask) for i in range(count) if i ^ mask < count]
    )


def plain(x_tokens, sign_bits, weight, upstream):
    panel_width = x_tokens.shape[1]
    groups = lax.axis_size("tensor")
    factor = 1.0 / math.sqrt(panel_width * groups)
    column_sign = (1 - 2 * sign_bits).astype(jnp.bfloat16)
    current = jnp.dot(
        x_tokens * column_sign[None, :],
        hadamard(panel_width),
        preferred_element_type=jnp.float32,
    )
    position = lax.axis_index("tensor")
    for section_bit in range(groups.bit_length() - 1):
        partner = swap(current.astype(jnp.bfloat16), "tensor", 1 << section_bit).astype(
            current.dtype
        )
        upper_half = position >> section_bit & 1 == 1
        current = jnp.where(upper_half, partner - current, current + partner)
    quantized = (current * factor).astype(jnp.bfloat16)
    gathered = lax.all_gather(quantized, "dp", axis=0, tiled=True)
    projected = lax.psum_scatter(
        jnp.dot(gathered, weight, preferred_element_type=jnp.float32).astype(jnp.bfloat16),
        "tensor",
        scatter_dimension=0,
        tiled=True,
    )
    weight_grad = lax.dot_general(
        gathered,
        lax.all_gather(upstream, "tensor", axis=0, tiled=True),
        (((0,), (0,)), ((), ())),
        preferred_element_type=jnp.float32,
    )
    return (projected, weight_grad)


def parity_sign(bits):
    return (1 - 2 * ((bits ^ bits >> 1) & 1)).astype(jnp.float32)


def butterfly(parts):
    stride = 1
    parts = list(parts)
    while stride < len(parts):
        for low in range(len(parts)):
            if not low & stride:
                a, b = parts[low], parts[low | stride]
                parts[low], parts[low | stride] = a + b, a - b
        stride *= 2
    return parts


def whole(shape):
    return pl.BlockSpec(shape, lambda n: (0,) * len(shape))


def tile_of(width, first=0):
    return next((t for t in (512, 256, 128) if width % t == 0 and first % t == 0), width)


def after(arrays, *earlier):
    arrays = list(arrays)
    return list(lax.optimization_barrier(tuple(arrays) + tuple(earlier))[: len(arrays)])


def sign_kernel(x_ref, bits_ref, *outs):
    z = lax.axis_index("tensor")
    rows = outs[0].shape[0]
    sign = (1 - 2 * bits_ref[...]).astype(jnp.float32)
    for m, out in enumerate(outs):
        first = pl.multiple_of((z ^ m) * rows, rows)
        out[...] = (x_ref[pl.ds(first, rows), :].astype(jnp.float32) * sign).astype(out.dtype)


def signed_pieces(x, sign_bits, groups):
    rows, width = x.shape
    part = rows // groups
    return pl.pallas_call(
        sign_kernel,
        out_shape=[jax.ShapeDtypeStruct((part, width), jnp.bfloat16)] * groups,
        in_specs=[VMEM] * 2,
        out_specs=[VMEM] * groups,
        compiler_params=pltpu.CompilerParams(vmem_limit_bytes=8 * MIB),
        name="signed_pieces",
    )(x, sign_bits.reshape(1, width))


def rotate_kernel(groups, order, factor, h_ref, *refs):
    pieces, outs = refs[:groups], refs[groups:]
    z = lax.axis_index("tensor")
    rows, width = pieces[0].shape
    chunks = width // order
    stacked = jnp.concatenate(
        [piece[:, j * order : (j + 1) * order] for piece in pieces for j in range(chunks)], axis=0
    )
    product = jnp.dot(stacked, h_ref[...], preferred_element_type=jnp.float32)
    rotated = []
    for i in range(groups):
        sign = parity_sign(z & i)
        rotated.append(
            butterfly(
                [
                    product[(i * chunks + j) * rows : (i * chunks + j + 1) * rows] * sign
                    for j in range(chunks)
                ]
            )
        )
    for j in range(chunks):
        panel = butterfly([r[j] for r in rotated])
        for m in range(groups):
            scale = parity_sign((z ^ m) & z) * factor
            outs[m][:, j * order : (j + 1) * order] = (panel[m] * scale).astype(jnp.bfloat16)


def rotate(pieces):
    groups = len(pieces)
    rows, width = pieces[0].shape
    order = min(256, width)
    return pl.pallas_call(
        functools.partial(rotate_kernel, groups, order, 1.0 / math.sqrt(width * groups)),
        out_shape=[jax.ShapeDtypeStruct((rows, width), jnp.bfloat16)] * groups,
        in_specs=[VMEM] * (1 + groups),
        out_specs=[VMEM] * groups,
        compiler_params=pltpu.CompilerParams(vmem_limit_bytes=8 * MIB),
        name="rotate",
    )(hadamard(order), *pieces)


def gather_rows(own, d):
    x, y, core = swap(own, "dp", 2), swap(own, "dp", 4), swap(own, "dp", 1)
    x, y = after([x, y])
    through = jnp.where(d & 1 == 0, x, y)
    diagonal = lax.ppermute(
        through, "dp", [(i, i ^ (4 if i & 1 == 0 else 2)) for i in range(8)]
    )
    return [
        own,
        core,
        x,
        swap(x, "dp", 1),
        y,
        swap(y, "dp", 1),
        diagonal,
        swap(diagonal, "dp", 1),
    ]


def is_outer(z):
    return 1 - ((z ^ z >> 1) & 1)


def slot(m, z):
    return m ^ (m >> 1 & is_outer(z))


def first_kernel(*refs):
    pieces, (w_ref, q_ref, *out_refs, sems) = refs[:8], refs[8:]
    rows = pieces[0].shape[0]

    @pl.when(pl.program_id(0) == 0)
    def _():
        z, d = lax.axis_index("tensor"), lax.axis_index("dp")
        copies = []
        for mask, piece in enumerate(pieces):
            start = slot(((d ^ mask) >> 1) ^ z, z) * (2 * rows) + ((d ^ mask) & 1) * rows
            copies.append(
                pltpu.make_async_copy(
                    piece, q_ref.at[pl.ds(pl.multiple_of(start, rows), rows), :], sems.at[mask]
                )
            )
        for copy in copies:
            copy.start()
        for copy in copies:
            copy.wait()

    project_kernel(q_ref, w_ref, *out_refs)


def project_kernel(q_ref, w_ref, *out_refs):
    product = jnp.dot(q_ref[...], w_ref[...], preferred_element_type=jnp.float32)
    first = 0
    for out_ref in out_refs:
        rows = out_ref.shape[0]
        out_ref[...] = product[first : first + rows].astype(out_ref.dtype)
        first += rows


def project_first(pieces, weight, width, blocks):
    depth = weight.shape[0]
    tokens = sum(blocks)
    tile = tile_of(width)
    q, *products = pl.pallas_call(
        first_kernel,
        out_shape=[
            jax.ShapeDtypeStruct((tokens, depth), jnp.bfloat16),
            *[jax.ShapeDtypeStruct((block, width), jnp.bfloat16) for block in blocks],
        ],
        grid=(width // tile,),
        in_specs=[pl.BlockSpec(memory_space=pl.ANY)] * len(pieces)
        + [pl.BlockSpec((depth, tile), lambda n: (0, n))],
        out_specs=[whole((tokens, depth))]
        + [pl.BlockSpec((block, tile), lambda n: (0, n)) for block in blocks],
        scratch_shapes=[pltpu.SemaphoreType.DMA((len(pieces),))],
        compiler_params=pltpu.CompilerParams(vmem_limit_bytes=48 * MIB),
        cost_estimate=pl.CostEstimate(flops=1, bytes_accessed=1, transcendentals=0),
        name="project_first",
    )(*pieces, weight)
    return q, products


def project(q, weight, first, width, blocks):
    tile = tile_of(width, first)
    tokens, depth = q.shape
    return pl.pallas_call(
        project_kernel,
        out_shape=[jax.ShapeDtypeStruct((block, width), jnp.bfloat16) for block in blocks],
        grid=(width // tile,),
        in_specs=[
            whole((tokens, depth)),
            pl.BlockSpec((depth, tile), lambda n: (0, n + first // tile)),
        ],
        out_specs=[pl.BlockSpec((block, tile), lambda n: (0, n)) for block in blocks],
        compiler_params=pltpu.CompilerParams(vmem_limit_bytes=48 * MIB),
        cost_estimate=pl.CostEstimate(
            flops=2 * tokens * depth * width,
            bytes_accessed=2 * (tokens * depth + depth * width + tokens * width),
            transcendentals=0,
        ),
        name="project",
    )(q, weight)


def transpose_kernel(q_ref, out_ref):
    out_ref[...] = q_ref[...].T


def transposed(q):
    tokens, depth = q.shape
    return pl.pallas_call(
        transpose_kernel,
        out_shape=jax.ShapeDtypeStruct((depth, tokens), jnp.bfloat16),
        in_specs=[VMEM],
        out_specs=VMEM,
        compiler_params=pltpu.CompilerParams(vmem_limit_bytes=16 * MIB),
        name="transposed",
    )(q)


def grad_kernel(tile, start, q_t, own_ref, e1, o1, o2, e2, e3, *refs):
    out_ref, up_all, sems = refs[-3:]
    z = lax.axis_index("tensor")
    rows, width = own_ref.shape[0], up_all.shape[1]

    @pl.when(pl.program_id(0) == 0)
    def _():
        def copy(source, m):
            return pltpu.make_async_copy(
                source.at[:, start : start + width],
                up_all.at[m * rows : (m + 1) * rows, :],
                sems.at[m],
            )

        copy(own_ref, 0).start()
        copy(e1, 1).start()

        @pl.when(is_outer(z) == 0)
        def _():
            copy(o2, 2).start()
            copy(o1, 3).start()

        @pl.when(is_outer(z) == 1)
        def _():
            copy(e3, 2).start()
            copy(e2, 3).start()

        for m in range(4):
            copy(own_ref, m).wait()

    first = pl.multiple_of(pl.program_id(0) * tile, tile)
    out_ref[...] = jnp.dot(
        q_t[...], up_all[:, pl.ds(first, tile)], preferred_element_type=jnp.float32
    )


def weight_gradient(q_t, own, moved, start, width, done=None):
    depth, tokens = q_t.shape
    hidden = own.shape[1]
    tile = tile_of(width, start)
    before = [] if done is None else [done]
    anywhere = pl.BlockSpec(memory_space=pl.ANY)
    return pl.pallas_call(
        functools.partial(grad_kernel, tile, start),
        out_shape=jax.ShapeDtypeStruct((depth, hidden), jnp.float32),
        grid=(width // tile,),
        in_specs=[whole((depth, tokens))] + [anywhere] * (6 + len(before)),
        out_specs=pl.BlockSpec((depth, tile), lambda n: (0, n + start // tile)),
        input_output_aliases={7: 0} if before else {},
        scratch_shapes=[
            pltpu.VMEM((tokens, width), jnp.bfloat16),
            pltpu.SemaphoreType.DMA((4,)),
        ],
        compiler_params=pltpu.CompilerParams(vmem_limit_bytes=28 * MIB),
        cost_estimate=pl.CostEstimate(
            flops=2 * tokens * depth * width,
            bytes_accessed=2 * tokens * (depth + width) + 4 * depth * width,
            transcendentals=0,
        ),
        name="weight_gradient",
    )(q_t, own, *moved, *before)


def total(*blocks):
    return sum(b.astype(jnp.float32) for b in blocks).astype(jnp.bfloat16)


def move(block, *pairs):
    return lax.ppermute(block, "tensor", pairs)


INWARD = ((0, 1), (3, 2))
MIDDLE = ((1, 2), (2, 1))
OUTWARD = ((1, 0), (2, 3))


def lined(x_tokens, sign_bits, weight, upstream):
    groups = lax.axis_size("tensor")
    z = lax.axis_index("tensor")
    d = lax.axis_index("dp")
    rows = x_tokens.shape[0]
    hidden = weight.shape[1]

    pieces = list(signed_pieces(x_tokens, sign_bits, groups))
    for m in (3, 2, 1):
        pieces[m] = swap(pieces[m], "tensor", m)
    turned = list(rotate(pieces))
    (up,) = after([upstream], turned[0])
    for m in (3, 2, 1):
        turned[m] = swap(turned[m], "tensor", m)
    own = jnp.concatenate(
        [lax.select_n(z, *[turned[g ^ k] for k in range(groups)]) for g in range(groups)]
    )

    e1 = swap(up, "tensor", 1)
    o1 = move(up, *MIDDLE)

    gathered = gather_rows(own, d)
    cut = 3 * hidden // 7 // 512 * 512
    block = rows * len(gathered) // groups
    q, *first = project_first(gathered, weight, cut, (block, block, 2 * block))
    own_a, pair_a, beyond_a = first[0]
    q, e1, o1 = after([q, e1, o1])
    o2 = move(e1, *MIDDLE)
    e2 = move(o1, *OUTWARD)
    own_b, pair_b, far_b, near_b = project(q, weight, cut, hidden - cut, (block,) * 4)

    inward_a = move(beyond_a, *INWARD)
    inward_far = move(far_b, *INWARD)
    (inward_near,) = after([near_b], inward_a)
    inward_near = move(inward_near, *INWARD)
    across_a = move(total(beyond_a, inward_a), *MIDDLE)
    o2, e2 = after([o2, e2], inward_a)
    e3 = move(o2, *OUTWARD)
    inward_far, o2, e2 = after([inward_far, o2, e2])
    across_far = move(total(far_b, inward_far), *MIDDLE)
    out_a = swap(total(pair_a, across_a[:block]), "tensor", 1)

    (late,) = after([q], inward_far)
    q_t = transposed(late)
    moved = (e1, o1, o2, e2, e3)
    some = hidden // 2 // 512 * 512
    (late,) = after([q_t], across_a)
    grad = weight_gradient(late, upstream, moved, 0, some)

    inward_near, grad = after([inward_near, grad])
    across_near = move(total(near_b, inward_near), *MIDDLE)
    across_far, grad, out_a = after([across_far, grad, out_a])
    out_b = swap(total(pair_b, across_far), "tensor", 1)
    (late,) = after([q_t], across_far)
    weight_grad = weight_gradient(late, upstream, moved, some, hidden - some, grad)
    projected = jnp.concatenate(
        [total(own_a, out_a, across_a[block:]), total(own_b, out_b, across_near)], axis=1
    )
    return (projected, weight_grad)


def per_device(x_tokens, sign_bits, weight, upstream):
    rows, width = x_tokens.shape
    hidden = weight.shape[1]
    fits = rows % 64 == 0 and width % 256 == 0 and hidden % 512 == 0 and hidden >= 1536
    if (lax.axis_size("dp"), lax.axis_size("tensor")) == (8, 4) and fits:
        return lined(x_tokens, sign_bits, weight, upstream)
    return plain(x_tokens, sign_bits, weight, upstream)


def solution(mesh):
    in_specs = (P("dp", "tensor"), P("tensor"), P("tensor", "dp"), P("tensor", "dp"))
    out_specs = (P("tensor", "dp"), P("tensor", "dp"))
    return jax.shard_map(
        per_device, mesh=mesh, in_specs=in_specs, out_specs=out_specs, check_vma=False
    )
```

profile of v0, /device:TPU:0, one launch (start us, length us, event | category | flops | bytes accessed | tf_op | source)
XLA Modules:
  0.0 116.2 jit_solution(10897684927209297610)
XLA Ops:
  0.6 1.0 copy-done.1
  1.7 0.7 copy-done.2
  2.4 0.1 signed_pieces.1
  2.4 3.1 %collective-permute-start = (bf16[16,2048]{1,0:T(8,128)(2,1)S(1)}, bf16[16,2048]{1,0:T(8,128)(2,1)S(1)}, u32[]{:S(2)}, u32[]{:S(2)}) collective-permute-start(bf16[16,2048]{1,0:T(8,128)(2,1)S(1)} %get-tuple-element.39), channel_id=1, source_target_pairs={{0,1},{1,0},{2,3},{3,2},{4,5},{5,4},{6,7},{7,6},{8,9},{9,8},{10,11... | collective-permute-start | bytes 196616 | tf_op jit(solution)/shard_map/ppermute | solution.py:27
  5.5 2.6 %collective-permute-start.1 = (bf16[16,2048]{1,0:T(8,128)(2,1)S(1)}, bf16[16,2048]{1,0:T(8,128)(2,1)S(1)}, u32[]{:S(2)}, u32[]{:S(2)}) collective-permute-start(bf16[16,2048]{1,0:T(8,128)(2,1)S(1)} %get-tuple-element.40), channel_id=1, source_target_pairs={{0,2},{1,3},{2,0},{3,1},{4,6},{5,7},{6,4},{7,5},{8,10},{9,11},{10,... | collective-permute-start | bytes 196616 | tf_op jit(solution)/shard_map/ppermute | solution.py:27
  8.1 0.0 collective-permute-start.2
  8.1 0.3 fusion.3.h_ref
  8.4 0.0 collective-permute-done.refs_1_
  8.5 4.3 %collective-permute-done.1.refs_2_ = bf16[16,2048]{1,0:T(8,128)(2,1)S(1)} collective-permute-done((bf16[16,2048]{1,0:T(8,128)(2,1)S(1)}, bf16[16,2048]{1,0:T(8,128)(2,1)S(1)}, u32[]{:S(2)}, u32[]{:S(2)}) %collective-permute-start.1) | collective-permute-done | bytes 65568 | tf_op jit(solution)/shard_map/ppermute | solution.py:27
  12.8 1.4 %collective-permute-done.2.refs_3_ = bf16[16,2048]{1,0:T(8,128)(2,1)S(1)} collective-permute-done((bf16[16,2048]{1,0:T(8,128)(2,1)S(1)}, bf16[16,2048]{1,0:T(8,128)(2,1)S(1)}, u32[]{:S(2)}, u32[]{:S(2)}) %collective-permute-start.2) | collective-permute-done | bytes 65568 | tf_op jit(solution)/shard_map/ppermute | solution.py:27
  14.2 0.3 rotate.1
  14.5 1.6 %collective-permute-start.4 = (bf16[16,2048]{1,0:T(8,128)(2,1)S(1)}, bf16[16,2048]{1,0:T(8,128)(2,1)S(1)}, u32[]{:S(2)}, u32[]{:S(2)}) collective-permute-start(bf16[16,2048]{1,0:T(8,128)(2,1)S(1)} %get-tuple-element.44), channel_id=1, source_target_pairs={{0,2},{1,3},{2,0},{3,1},{4,6},{5,7},{6,4},{7,5},{8,10},{9,11},{10,... | collective-permute-start | bytes 196616 | tf_op jit(solution)/shard_map/ppermute | solution.py:27
  16.1 0.7 collective-permute-start.5
  16.8 1.2 %collective-permute-start.3 = (bf16[16,2048]{1,0:T(8,128)(2,1)S(1)}, bf16[16,2048]{1,0:T(8,128)(2,1)S(1)}, u32[]{:S(2)}, u32[]{:S(2)}) collective-permute-start(bf16[16,2048]{1,0:T(8,128)(2,1)S(1)} %get-tuple-element.43), channel_id=1, source_target_pairs={{0,1},{1,0},{2,3},{3,2},{4,5},{5,4},{6,7},{7,6},{8,9},{9,8},{10,11... | collective-permute-start | bytes 196616 | tf_op jit(solution)/shard_map/ppermute | solution.py:27
  18.0 2.4 %collective-permute-done.4 = bf16[16,2048]{1,0:T(8,128)(2,1)S(1)} collective-permute-done((bf16[16,2048]{1,0:T(8,128)(2,1)S(1)}, bf16[16,2048]{1,0:T(8,128)(2,1)S(1)}, u32[]{:S(2)}, u32[]{:S(2)}) %collective-permute-start.4) | collective-permute-done | bytes 65568 | tf_op jit(solution)/shard_map/ppermute | solution.py:27
  20.5 1.7 %collective-permute-done.5 = bf16[16,2048]{1,0:T(8,128)(2,1)S(1)} collective-permute-done((bf16[16,2048]{1,0:T(8,128)(2,1)S(1)}, bf16[16,2048]{1,0:T(8,128)(2,1)S(1)}, u32[]{:S(2)}, u32[]{:S(2)}) %collective-permute-start.5) | collective-permute-done | bytes 65568 | tf_op jit(solution)/shard_map/ppermute | solution.py:27
  22.2 0.0 collective-permute-done.3
  22.3 1.6 %collective-permute-start.7 = (bf16[64,2048]{1,0:T(8,128)(2,1)S(1)}, bf16[64,2048]{1,0:T(8,128)(2,1)S(1)}, u32[]{:S(2)}, u32[]{:S(2)}) collective-permute-start(bf16[64,2048]{1,0:T(8,128)(2,1)S(1)} %pad_maximum_fusion.1.refs_0_), channel_id=1, source_target_pairs={{0,8},{4,12},{8,0},{12,4},{16,24},{20,28},{24,16},{28,20},{1,9},{5... | collective-permute-start | bytes 786440 | tf_op jit(solution)/shard_map/ppermute | solution.py:27
  23.8 1.5 %collective-permute-start.8 = (bf16[64,2048]{1,0:T(8,128)(2,1)S(1)}, bf16[64,2048]{1,0:T(8,128)(2,1)S(1)}, u32[]{:S(2)}, u32[]{:S(2)}) collective-permute-start(bf16[64,2048]{1,0:T(8,128)(2,1)S(1)} %pad_maximum_fusion.1.refs_0_), channel_id=1, source_target_pairs={{0,16},{4,20},{8,24},{12,28},{16,0},{20,4},{24,8},{28,12},{1,17},{... | collective-permute-start | bytes 786440 | tf_op jit(solution)/shard_map/ppermute | solution.py:27
  25.4 0.1 collective-permute-start.13
  25.5 0.7 collective-permute-start.14
  26.2 0.1 collective-permute-start.6
  26.3 2.5 %collective-permute-done.7.refs_2_ = bf16[64,2048]{1,0:T(8,128)(2,1)S(1)} collective-permute-done((bf16[64,2048]{1,0:T(8,128)(2,1)S(1)}, bf16[64,2048]{1,0:T(8,128)(2,1)S(1)}, u32[]{:S(2)}, u32[]{:S(2)}) %collective-permute-start.7) | collective-permute-done | bytes 262176 | tf_op jit(solution)/shard_map/ppermute | solution.py:27
  28.7 1.5 %collective-permute-done.8.refs_4_ = bf16[64,2048]{1,0:T(8,128)(2,1)S(1)} collective-permute-done((bf16[64,2048]{1,0:T(8,128)(2,1)S(1)}, bf16[64,2048]{1,0:T(8,128)(2,1)S(1)}, u32[]{:S(2)}, u32[]{:S(2)}) %collective-permute-start.8) | collective-permute-done | bytes 262176 | tf_op jit(solution)/shard_map/ppermute | solution.py:27
  30.2 1.6 %collective-permute-start.11 = (bf16[64,2048]{1,0:T(8,128)(2,1)S(1)}, bf16[64,2048]{1,0:T(8,128)(2,1)S(1)}, u32[]{:S(2)}, u32[]{:S(2)}) collective-permute-start(bf16[64,2048]{1,0:T(8,128)(2,1)S(1)} %broadcast_select_fusion), channel_id=1, source_target_pairs={{0,16},{4,12},{8,24},{12,4},{16,0},{20,28},{24,8},{28,20},{1,17},{... | collective-permute-start | bytes 786440 | tf_op jit(solution)/shard_map/ppermute | solution.py:162
  31.8 0.0 collective-permute-start.9
  31.8 0.0 collective-permute-done.6.refs_1_
  31.8 0.5 collective-permute-start.10
  32.3 4.3 %collective-permute-done.11.refs_6_ = bf16[64,2048]{1,0:T(8,128)(2,1)S(1)} collective-permute-done((bf16[64,2048]{1,0:T(8,128)(2,1)S(1)}, bf16[64,2048]{1,0:T(8,128)(2,1)S(1)}, u32[]{:S(2)}, u32[]{:S(2)}) %collective-permute-start.11) | collective-permute-done | bytes 262176 | tf_op jit(solution)/shard_map/ppermute | solution.py:162
  36.7 0.0 collective-permute-start.12
  36.7 0.0 collective-permute-done.9.refs_3_
  36.7 0.0 collective-permute-done.10.refs_5_
  36.7 1.5 %collective-permute-done.12.refs_7_ = bf16[64,2048]{1,0:T(8,128)(2,1)S(1)} collective-permute-done((bf16[64,2048]{1,0:T(8,128)(2,1)S(1)}, bf16[64,2048]{1,0:T(8,128)(2,1)S(1)}, u32[]{:S(2)}, u32[]{:S(2)}) %collective-permute-start.12) | collective-permute-done | bytes 262176 | tf_op jit(solution)/shard_map/ppermute | solution.py:27
  38.2 6.0 %project_first.1 = (bf16[512,2048]{1,0:T(8,128)(2,1)S(1)}, bf16[128,1536]{1,0:T(8,128)(2,1)S(1)}, bf16[128,1536]{1,0:T(8,128)(2,1)S(1)}, bf16[256,1536]{1,0:T(8,128)(2,1)S(1)}) custom-call(bf16[64,2048]{1,0:T(8,128)(2,1)S(1)} %pad_maximum_fusion.1.refs_0_, bf16[64,2048]{1,0:T(8,128)(2,1)S(1)} %collective-permute-done.6.refs_1_, ...), custom_call_target="tpu_custom_call" | custom-call | flops 1 | bytes 1 | tf_op jit(solution)/shard_map/project_first/pallas_call | solution.py:221
  44.2 2.3 %collective-permute-start.18 = (bf16[256,1536]{1,0:T(8,128)(2,1)S(1)}, bf16[256,1536]{1,0:T(8,128)(2,1)S(1)}, u32[]{:S(2)}, u32[]{:S(2)}) collective-permute-start(bf16[256,1536]{1,0:T(8,128)(2,1)S(1)} %get-tuple-element.55), channel_id=1, source_target_pairs={{0,1},{3,2},{4,5},{7,6},{8,9},{11,10},{12,13},{15,14},{16,17},{19,... | collective-permute-start | bytes 2359304 | tf_op jit(solution)/shard_map/ppermute | solution.py:346
  46.5 0.0 collective-permute-done.13.e1
  46.5 0.7 collective-permute-start.16
  47.3 1.3 %collective-permute-start.17 = (bf16[128,3584]{1,0:T(8,128)(2,1)S(1)}, bf16[128,3584]{1,0:T(8,128)(2,1)S(1)}, u32[]{:S(2)}, u32[]{:S(2)}) collective-permute-start(bf16[128,3584]{1,0:T(8,128)(2,1)S(1)} %collective-permute-done.14.o1), channel_id=1, source_target_pairs={{1,0},{2,3},{5,4},{6,7},{9,8},{10,11},{13,12},{14,15},{17,16},{18,... | collective-permute-start | bytes 2752520 | tf_op jit(solution)/shard_map/ppermute | solution.py:346
  48.6 7.1 %project.1 = (bf16[128,2048]{1,0:T(8,128)(2,1)S(1)}, bf16[128,2048]{1,0:T(8,128)(2,1)S(1)}, bf16[128,2048]{1,0:T(8,128)(2,1)S(1)}, bf16[128,2048]{1,0:T(8,128)(2,1)S(1)}) custom-call(bf16[512,2048]{1,0:T(8,128)(2,1)S(1)} %get-tuple-element.61.q_ref, bf16[2048,3584]{1,0:T(8,128)(2,1)} %w_ref.1), custom_call_target="tpu_custom_call" | custom-call | flops 4294967296 | bytes 12582912 | tf_op jit(solution)/shard_map/project/pallas_call | solution.py:243
  55.7 6.3 %collective-permute-start.15 = (bf16[128,2048]{1,0:T(8,128)(2,1)S(1)}, bf16[128,2048]{1,0:T(8,128)(2,1)S(1)}, u32[]{:S(2)}, u32[]{:S(2)}) collective-permute-start(bf16[128,2048]{1,0:T(8,128)(2,1)S(1)} %get-tuple-element.52), channel_id=1, source_target_pairs={{0,1},{3,2},{4,5},{7,6},{8,9},{11,10},{12,13},{15,14},{16,17},{19,... | collective-permute-start | bytes 1572872 | tf_op jit(solution)/shard_map/ppermute | solution.py:346
  62.0 2.3 %collective-permute-done.18 = bf16[256,1536]{1,0:T(8,128)(2,1)S(1)} collective-permute-done((bf16[256,1536]{1,0:T(8,128)(2,1)S(1)}, bf16[256,1536]{1,0:T(8,128)(2,1)S(1)}, u32[]{:S(2)}, u32[]{:S(2)}) %collective-permute-start.18) | collective-permute-done | bytes 786464 | tf_op jit(solution)/shard_map/ppermute | solution.py:346
  64.4 0.2 add_convert_fusion
  64.5 0.7 collective-permute-start.21
  65.3 7.1 %collective-permute-start.20 = (bf16[128,2048]{1,0:T(8,128)(2,1)S(1)}, bf16[128,2048]{1,0:T(8,128)(2,1)S(1)}, u32[]{:S(2)}, u32[]{:S(2)}) collective-permute-start(bf16[128,2048]{1,0:T(8,128)(2,1)S(1)} %get-tuple-element.60), channel_id=1, source_target_pairs={{0,1},{3,2},{4,5},{7,6},{8,9},{11,10},{12,13},{15,14},{16,17},{19,... | collective-permute-start | bytes 1572872 | tf_op jit(solution)/shard_map/ppermute | solution.py:346
  72.4 0.0 collective-permute-done.17.e2
  72.4 1.3 %collective-permute-start.22 = (bf16[128,3584]{1,0:T(8,128)(2,1)S(1)}, bf16[128,3584]{1,0:T(8,128)(2,1)S(1)}, u32[]{:S(2)}, u32[]{:S(2)}) collective-permute-start(bf16[128,3584]{1,0:T(8,128)(2,1)S(1)} %collective-permute-done.16.o2), channel_id=1, source_target_pairs={{1,0},{2,3},{5,4},{6,7},{9,8},{10,11},{13,12},{14,15},{17,16},{18,... | collective-permute-start | bytes 2752520 | tf_op jit(solution)/shard_map/ppermute | solution.py:346
  73.7 1.9 %collective-permute-done.15 = bf16[128,2048]{1,0:T(8,128)(2,1)S(1)} collective-permute-done((bf16[128,2048]{1,0:T(8,128)(2,1)S(1)}, bf16[128,2048]{1,0:T(8,128)(2,1)S(1)}, u32[]{:S(2)}, u32[]{:S(2)}) %collective-permute-start.15) | collective-permute-done | bytes 524320 | tf_op jit(solution)/shard_map/ppermute | solution.py:346
  75.6 0.6 transposed.1.q_t
  76.2 0.1 add_convert_fusion.4
  76.3 0.7 collective-permute-start.19
  77.0 0.1 add_convert_fusion.6
  77.1 12.4 %collective-permute-start.23 = (bf16[128,1536]{1,0:T(8,128)(2,1)S(1)}, bf16[128,1536]{1,0:T(8,128)(2,1)S(1)}, u32[]{:S(2)}, u32[]{:S(2)}) collective-permute-start(bf16[128,1536]{1,0:T(8,128)(2,1)S(1)} %add_convert_fusion.6), channel_id=1, source_target_pairs={{0,1},{1,0},{2,3},{3,2},{4,5},{5,4},{6,7},{7,6},{8,9},{9,8},{10,11... | collective-permute-start | bytes 1179656 | tf_op jit(solution)/shard_map/ppermute | solution.py:27
  89.6 8.0 %collective-permute-done.22.e3 = bf16[128,3584]{1,0:T(8,128)(2,1)S(1)} collective-permute-done((bf16[128,3584]{1,0:T(8,128)(2,1)S(1)}, bf16[128,3584]{1,0:T(8,128)(2,1)S(1)}, u32[]{:S(2)}, u32[]{:S(2)}) %collective-permute-start.22) | collective-permute-done | bytes 917536 | tf_op jit(solution)/shard_map/ppermute | solution.py:346
  97.6 6.7 %weight_gradient.2.refs_0_ = f32[2048,3584]{1,0:T(8,128)} custom-call(bf16[2048,512]{1,0:T(8,128)(2,1)S(1)} %transposed.1.q_t, bf16[128,3584]{1,0:T(8,128)(2,1)S(1)} %copy-done, bf16[128,3584]{1,0:T(8,128)(2,1)S(1)} %collective-permute-done.13.e1, bf16[128,3584]{1,0:T(8,128)(2,1)S(1)} %collective-permute-done.14.o1, ...), custom_call_target="tpu_custom_call" | custom-call | flops 3221225472 | bytes 16252928 | tf_op jit(solution)/shard_map/weight_gradient/pallas_call | solution.py:320
  104.3 0.0 collective-permute-done.20
  104.3 0.1 add_convert_fusion.2
  104.5 0.7 collective-permute-start.25
  105.2 0.1 add_convert_fusion.3
  105.3 1.3 %collective-permute-start.24 = (bf16[128,2048]{1,0:T(8,128)(2,1)S(1)}, bf16[128,2048]{1,0:T(8,128)(2,1)S(1)}, u32[]{:S(2)}, u32[]{:S(2)}) collective-permute-start(bf16[128,2048]{1,0:T(8,128)(2,1)S(1)} %add_convert_fusion.3), channel_id=1, source_target_pairs={{0,1},{1,0},{2,3},{3,2},{4,5},{5,4},{6,7},{7,6},{8,9},{9,8},{10,11... | collective-permute-start | bytes 1572872 | tf_op jit(solution)/shard_map/ppermute | solution.py:27
  106.7 8.1 %weight_gradient.3 = f32[2048,3584]{1,0:T(8,128)} custom-call(bf16[2048,512]{1,0:T(8,128)(2,1)S(1)} %transposed.1.q_t, bf16[128,3584]{1,0:T(8,128)(2,1)S(1)} %copy-done, bf16[128,3584]{1,0:T(8,128)(2,1)S(1)} %collective-permute-done.13.e1, bf16[128,3584]{1,0:T(8,128)(2,1)S(1)} %collective-permute-done.14.o1, ...), custom_call_target="tpu_custom_call", output_to_operand_aliasing={{}: (7, {})} | custom-call | flops 4294967296 | bytes 20971520 | tf_op jit(solution)/shard_map/weight_gradient/pallas_call | solution.py:320
  114.8 0.1 add_convert_fusion.5
  114.9 0.0 collective-permute-done.25
  114.9 0.2 add_convert_fusion.1
  115.2 1.0 pad_maximum_fusion
  (13 shorter events, 0.1 us)
Async XLA Ops:
  0.6 24.7 %copy-start = (bf16[128,3584]{1,0:T(8,128)(2,1)S(1)}, bf16[128,3584]{1,0:T(8,128)(2,1)}, u32[]{:S(2)}) copy-start(bf16[128,3584]{1,0:T(8,128)(2,1)} %own_ref.3) | copy-start | bytes 2752516
  0.6 1.0 copy-start.1
  1.7 0.7 copy-start.2
  2.4 6.0 %collective-permute-start = (bf16[16,2048]{1,0:T(8,128)(2,1)S(1)}, bf16[16,2048]{1,0:T(8,128)(2,1)S(1)}, u32[]{:S(2)}, u32[]{:S(2)}) collective-permute-start(bf16[16,2048]{1,0:T(8,128)(2,1)S(1)} %get-tuple-element.39), channel_id=1, source_target_pairs={{0,1},{1,0},{2,3},{3,2},{4,5},{5,4},{6,7},{7,6},{8,9},{9,8},{10,11... | collective-permute-start | bytes 196616 | tf_op jit(solution)/shard_map/ppermute | solution.py:27
  5.5 7.3 %collective-permute-start.1 = (bf16[16,2048]{1,0:T(8,128)(2,1)S(1)}, bf16[16,2048]{1,0:T(8,128)(2,1)S(1)}, u32[]{:S(2)}, u32[]{:S(2)}) collective-permute-start(bf16[16,2048]{1,0:T(8,128)(2,1)S(1)} %get-tuple-element.40), channel_id=1, source_target_pairs={{0,2},{1,3},{2,0},{3,1},{4,6},{5,7},{6,4},{7,5},{8,10},{9,11},{10,... | collective-permute-start | bytes 196616 | tf_op jit(solution)/shard_map/ppermute | solution.py:27
  8.1 6.1 %collective-permute-start.2 = (bf16[16,2048]{1,0:T(8,128)(2,1)S(1)}, bf16[16,2048]{1,0:T(8,128)(2,1)S(1)}, u32[]{:S(2)}, u32[]{:S(2)}) collective-permute-start(bf16[16,2048]{1,0:T(8,128)(2,1)S(1)} %get-tuple-element.41), channel_id=1, source_target_pairs={{0,3},{1,2},{2,1},{3,0},{4,7},{5,6},{6,5},{7,4},{8,11},{9,10},{10,... | collective-permute-start | bytes 196616 | tf_op jit(solution)/shard_map/ppermute | solution.py:27
  14.5 6.0 %collective-permute-start.4 = (bf16[16,2048]{1,0:T(8,128)(2,1)S(1)}, bf16[16,2048]{1,0:T(8,128)(2,1)S(1)}, u32[]{:S(2)}, u32[]{:S(2)}) collective-permute-start(bf16[16,2048]{1,0:T(8,128)(2,1)S(1)} %get-tuple-element.44), channel_id=1, source_target_pairs={{0,2},{1,3},{2,0},{3,1},{4,6},{5,7},{6,4},{7,5},{8,10},{9,11},{10,... | collective-permute-start | bytes 196616 | tf_op jit(solution)/shard_map/ppermute | solution.py:27
  16.1 6.1 %collective-permute-start.5 = (bf16[16,2048]{1,0:T(8,128)(2,1)S(1)}, bf16[16,2048]{1,0:T(8,128)(2,1)S(1)}, u32[]{:S(2)}, u32[]{:S(2)}) collective-permute-start(bf16[16,2048]{1,0:T(8,128)(2,1)S(1)} %get-tuple-element.45), channel_id=1, source_target_pairs={{0,3},{1,2},{2,1},{3,0},{4,7},{5,6},{6,5},{7,4},{8,11},{9,10},{10,... | collective-permute-start | bytes 196616 | tf_op jit(solution)/shard_map/ppermute | solution.py:27
  16.8 5.4 %collective-permute-start.3 = (bf16[16,2048]{1,0:T(8,128)(2,1)S(1)}, bf16[16,2048]{1,0:T(8,128)(2,1)S(1)}, u32[]{:S(2)}, u32[]{:S(2)}) collective-permute-start(bf16[16,2048]{1,0:T(8,128)(2,1)S(1)} %get-tuple-element.43), channel_id=1, source_target_pairs={{0,1},{1,0},{2,3},{3,2},{4,5},{5,4},{6,7},{7,6},{8,9},{9,8},{10,11... | collective-permute-start | bytes 196616 | tf_op jit(solution)/shard_map/ppermute | solution.py:27
  22.3 6.4 %collective-permute-start.7 = (bf16[64,2048]{1,0:T(8,128)(2,1)S(1)}, bf16[64,2048]{1,0:T(8,128)(2,1)S(1)}, u32[]{:S(2)}, u32[]{:S(2)}) collective-permute-start(bf16[64,2048]{1,0:T(8,128)(2,1)S(1)} %pad_maximum_fusion.1.refs_0_), channel_id=1, source_target_pairs={{0,8},{4,12},{8,0},{12,4},{16,24},{20,28},{24,16},{28,20},{1,9},{5... | collective-permute-start | bytes 786440 | tf_op jit(solution)/shard_map/ppermute | solution.py:27
  23.8 6.4 %collective-permute-start.8 = (bf16[64,2048]{1,0:T(8,128)(2,1)S(1)}, bf16[64,2048]{1,0:T(8,128)(2,1)S(1)}, u32[]{:S(2)}, u32[]{:S(2)}) collective-permute-start(bf16[64,2048]{1,0:T(8,128)(2,1)S(1)} %pad_maximum_fusion.1.refs_0_), channel_id=1, source_target_pairs={{0,16},{4,20},{8,24},{12,28},{16,0},{20,4},{24,8},{28,12},{1,17},{... | collective-permute-start | bytes 786440 | tf_op jit(solution)/shard_map/ppermute | solution.py:27
  25.4 21.2 %collective-permute-start.13 = (bf16[128,3584]{1,0:T(8,128)(2,1)S(1)}, bf16[128,3584]{1,0:T(8,128)(2,1)S(1)}, u32[]{:S(2)}, u32[]{:S(2)}) collective-permute-start(bf16[128,3584]{1,0:T(8,128)(2,1)S(1)} %copy-done), channel_id=1, source_target_pairs={{0,1},{1,0},{2,3},{3,2},{4,5},{5,4},{6,7},{7,6},{8,9},{9,8},{10,11... | collective-permute-start | bytes 2752520 | tf_op jit(solution)/shard_map/ppermute | solution.py:27
  25.5 21.1 %collective-permute-start.14 = (bf16[128,3584]{1,0:T(8,128)(2,1)S(1)}, bf16[128,3584]{1,0:T(8,128)(2,1)S(1)}, u32[]{:S(2)}, u32[]{:S(2)}) collective-permute-start(bf16[128,3584]{1,0:T(8,128)(2,1)S(1)} %copy-done), channel_id=1, source_target_pairs={{1,2},{2,1},{5,6},{6,5},{9,10},{10,9},{13,14},{14,13},{17,18},{18,... | collective-permute-start | bytes 2752520 | tf_op jit(solution)/shard_map/ppermute | solution.py:346
  26.2 5.7 %collective-permute-start.6 = (bf16[64,2048]{1,0:T(8,128)(2,1)S(1)}, bf16[64,2048]{1,0:T(8,128)(2,1)S(1)}, u32[]{:S(2)}, u32[]{:S(2)}) collective-permute-start(bf16[64,2048]{1,0:T(8,128)(2,1)S(1)} %pad_maximum_fusion.1.refs_0_), channel_id=1, source_target_pairs={{0,4},{4,0},{8,12},{12,8},{16,20},{20,16},{24,28},{28,24},{1,5},{5... | collective-permute-start | bytes 786440 | tf_op jit(solution)/shard_map/ppermute | solution.py:27
  30.2 6.4 %collective-permute-start.11 = (bf16[64,2048]{1,0:T(8,128)(2,1)S(1)}, bf16[64,2048]{1,0:T(8,128)(2,1)S(1)}, u32[]{:S(2)}, u32[]{:S(2)}) collective-permute-start(bf16[64,2048]{1,0:T(8,128)(2,1)S(1)} %broadcast_select_fusion), channel_id=1, source_target_pairs={{0,16},{4,12},{8,24},{12,4},{16,0},{20,28},{24,8},{28,20},{1,17},{... | collective-permute-start | bytes 786440 | tf_op jit(solution)/shard_map/ppermute | solution.py:162
  31.8 4.9 %collective-permute-start.9 = (bf16[64,2048]{1,0:T(8,128)(2,1)S(1)}, bf16[64,2048]{1,0:T(8,128)(2,1)S(1)}, u32[]{:S(2)}, u32[]{:S(2)}) collective-permute-start(bf16[64,2048]{1,0:T(8,128)(2,1)S(1)} %collective-permute-done.7.refs_2_), channel_id=1, source_target_pairs={{0,4},{4,0},{8,12},{12,8},{16,20},{20,16},{24,28},{28,24},{1,5},{5... | collective-permute-start | bytes 786440 | tf_op jit(solution)/shard_map/ppermute | solution.py:27
  31.8 4.9 %collective-permute-start.10 = (bf16[64,2048]{1,0:T(8,128)(2,1)S(1)}, bf16[64,2048]{1,0:T(8,128)(2,1)S(1)}, u32[]{:S(2)}, u32[]{:S(2)}) collective-permute-start(bf16[64,2048]{1,0:T(8,128)(2,1)S(1)} %collective-permute-done.8.refs_4_), channel_id=1, source_target_pairs={{0,4},{4,0},{8,12},{12,8},{16,20},{20,16},{24,28},{28,24},{1,5},{5... | collective-permute-start | bytes 786440 | tf_op jit(solution)/shard_map/ppermute | solution.py:27
  36.7 1.5 %collective-permute-start.12 = (bf16[64,2048]{1,0:T(8,128)(2,1)S(1)}, bf16[64,2048]{1,0:T(8,128)(2,1)S(1)}, u32[]{:S(2)}, u32[]{:S(2)}) collective-permute-start(bf16[64,2048]{1,0:T(8,128)(2,1)S(1)} %collective-permute-done.11.refs_6_), channel_id=1, source_target_pairs={{0,4},{4,0},{8,12},{12,8},{16,20},{20,16},{24,28},{28,24},{1,5},{5... | collective-permute-start | bytes 786440 | tf_op jit(solution)/shard_map/ppermute | solution.py:27
  44.2 20.1 %collective-permute-start.18 = (bf16[256,1536]{1,0:T(8,128)(2,1)S(1)}, bf16[256,1536]{1,0:T(8,128)(2,1)S(1)}, u32[]{:S(2)}, u32[]{:S(2)}) collective-permute-start(bf16[256,1536]{1,0:T(8,128)(2,1)S(1)} %get-tuple-element.55), channel_id=1, source_target_pairs={{0,1},{3,2},{4,5},{7,6},{8,9},{11,10},{12,13},{15,14},{16,17},{19,... | collective-permute-start | bytes 2359304 | tf_op jit(solution)/shard_map/ppermute | solution.py:346
  46.5 25.9 %collective-permute-start.16 = (bf16[128,3584]{1,0:T(8,128)(2,1)S(1)}, bf16[128,3584]{1,0:T(8,128)(2,1)S(1)}, u32[]{:S(2)}, u32[]{:S(2)}) collective-permute-start(bf16[128,3584]{1,0:T(8,128)(2,1)S(1)} %collective-permute-done.13.e1), channel_id=1, source_target_pairs={{1,2},{2,1},{5,6},{6,5},{9,10},{10,9},{13,14},{14,13},{17,18},{18,... | collective-permute-start | bytes 2752520 | tf_op jit(solution)/shard_map/ppermute | solution.py:346
  47.3 25.2 %collective-permute-start.17 = (bf16[128,3584]{1,0:T(8,128)(2,1)S(1)}, bf16[128,3584]{1,0:T(8,128)(2,1)S(1)}, u32[]{:S(2)}, u32[]{:S(2)}) collective-permute-start(bf16[128,3584]{1,0:T(8,128)(2,1)S(1)} %collective-permute-done.14.o1), channel_id=1, source_target_pairs={{1,0},{2,3},{5,4},{6,7},{9,8},{10,11},{13,12},{14,15},{17,16},{18,... | collective-permute-start | bytes 2752520 | tf_op jit(solution)/shard_map/ppermute | solution.py:346
  55.7 19.9 %collective-permute-start.15 = (bf16[128,2048]{1,0:T(8,128)(2,1)S(1)}, bf16[128,2048]{1,0:T(8,128)(2,1)S(1)}, u32[]{:S(2)}, u32[]{:S(2)}) collective-permute-start(bf16[128,2048]{1,0:T(8,128)(2,1)S(1)} %get-tuple-element.52), channel_id=1, source_target_pairs={{0,1},{3,2},{4,5},{7,6},{8,9},{11,10},{12,13},{15,14},{16,17},{19,... | collective-permute-start | bytes 1572872 | tf_op jit(solution)/shard_map/ppermute | solution.py:346
  64.5 12.5 %collective-permute-start.21 = (bf16[256,1536]{1,0:T(8,128)(2,1)S(1)}, bf16[256,1536]{1,0:T(8,128)(2,1)S(1)}, u32[]{:S(2)}, u32[]{:S(2)}) collective-permute-start(bf16[256,1536]{1,0:T(8,128)(2,1)S(1)} %add_convert_fusion), channel_id=1, source_target_pairs={{1,2},{2,1},{5,6},{6,5},{9,10},{10,9},{13,14},{14,13},{17,18},{18,... | collective-permute-start | bytes 2359304 | tf_op jit(solution)/shard_map/ppermute | solution.py:346
  65.3 39.0 %collective-permute-start.20 = (bf16[128,2048]{1,0:T(8,128)(2,1)S(1)}, bf16[128,2048]{1,0:T(8,128)(2,1)S(1)}, u32[]{:S(2)}, u32[]{:S(2)}) collective-permute-start(bf16[128,2048]{1,0:T(8,128)(2,1)S(1)} %get-tuple-element.60), channel_id=1, source_target_pairs={{0,1},{3,2},{4,5},{7,6},{8,9},{11,10},{12,13},{15,14},{16,17},{19,... | collective-permute-start | bytes 1572872 | tf_op jit(solution)/shard_map/ppermute | solution.py:346
  72.4 25.2 %collective-permute-start.22 = (bf16[128,3584]{1,0:T(8,128)(2,1)S(1)}, bf16[128,3584]{1,0:T(8,128)(2,1)S(1)}, u32[]{:S(2)}, u32[]{:S(2)}) collective-permute-start(bf16[128,3584]{1,0:T(8,128)(2,1)S(1)} %collective-permute-done.16.o2), channel_id=1, source_target_pairs={{1,0},{2,3},{5,4},{6,7},{9,8},{10,11},{13,12},{14,15},{17,16},{18,... | collective-permute-start | bytes 2752520 | tf_op jit(solution)/shard_map/ppermute | solution.py:346
  76.3 28.8 %collective-permute-start.19 = (bf16[128,2048]{1,0:T(8,128)(2,1)S(1)}, bf16[128,2048]{1,0:T(8,128)(2,1)S(1)}, u32[]{:S(2)}, u32[]{:S(2)}) collective-permute-start(bf16[128,2048]{1,0:T(8,128)(2,1)S(1)} %add_convert_fusion.4), channel_id=1, source_target_pairs={{1,2},{2,1},{5,6},{6,5},{9,10},{10,9},{13,14},{14,13},{17,18},{18,... | collective-permute-start | bytes 1572872 | tf_op jit(solution)/shard_map/ppermute | solution.py:346
  77.1 28.0 %collective-permute-start.23 = (bf16[128,1536]{1,0:T(8,128)(2,1)S(1)}, bf16[128,1536]{1,0:T(8,128)(2,1)S(1)}, u32[]{:S(2)}, u32[]{:S(2)}) collective-permute-start(bf16[128,1536]{1,0:T(8,128)(2,1)S(1)} %add_convert_fusion.6), channel_id=1, source_target_pairs={{0,1},{1,0},{2,3},{3,2},{4,5},{5,4},{6,7},{7,6},{8,9},{9,8},{10,11... | collective-permute-start | bytes 1179656 | tf_op jit(solution)/shard_map/ppermute | solution.py:27
  104.5 10.5 %collective-permute-start.25 = (bf16[128,2048]{1,0:T(8,128)(2,1)S(1)}, bf16[128,2048]{1,0:T(8,128)(2,1)S(1)}, u32[]{:S(2)}, u32[]{:S(2)}) collective-permute-start(bf16[128,2048]{1,0:T(8,128)(2,1)S(1)} %add_convert_fusion.2), channel_id=1, source_target_pairs={{1,2},{2,1},{5,6},{6,5},{9,10},{10,9},{13,14},{14,13},{17,18},{18,... | collective-permute-start | bytes 1572872 | tf_op jit(solution)/shard_map/ppermute | solution.py:346
  105.3 9.6 %collective-permute-start.24 = (bf16[128,2048]{1,0:T(8,128)(2,1)S(1)}, bf16[128,2048]{1,0:T(8,128)(2,1)S(1)}, u32[]{:S(2)}, u32[]{:S(2)}) collective-permute-start(bf16[128,2048]{1,0:T(8,128)(2,1)S(1)} %add_convert_fusion.3), channel_id=1, source_target_pairs={{0,1},{1,0},{2,3},{3,2},{4,5},{5,4},{6,7},{7,6},{8,9},{9,8},{10,11... | collective-permute-start | bytes 1572872 | tf_op jit(solution)/shard_map/ppermute | solution.py:27
where the time goes:
time: 117 us; the launch traced here: 116 us
  starting transfers between devices  50.1 us (43%)
  waiting for transfers between devices  32 us (27%)
  Pallas kernels  28.9 us (25%)
  other arithmetic  2.45 us (2%)
  local copies, waits for them, and re-layouts  1.72 us (1%)
    ppermute x15, starting transfers between devices, swap(): lax.ppermute(block, axis, [(i, i ^ mask) for i in range(count) if i ^ mas...  26.8 us
    ppermute x10, starting transfers between devices, move(): return lax.ppermute(block, 'tensor', pairs)  21.8 us
    ppermute x15, waiting for transfers between devices, swap(): lax.ppermute(block, axis, [(i, i ^ mask) for i in range(count) if i ^ mas...  15.4 us
    pallas_call x2, Pallas kernels, weight_gradient(): pl.pallas_call(functools.partial(grad_kernel, tile, start), out_shape=jax...  14.8 us
    ppermute x10, waiting for transfers between devices, move(): return lax.ppermute(block, 'tensor', pairs)  12.3 us
    pallas_call x1, Pallas kernels, project(): pl.pallas_call(project_kernel, out_shape=[jax.ShapeDtypeStruct((block, wi...  7.14 us
    pallas_call x1, Pallas kernels, project_first(): pl.pallas_call(first_kernel, out_shape=[jax.ShapeDtypeStruct((tokens, dep...  6.03 us
    ppermute x1, waiting for transfers between devices, gather_rows(): lax.ppermute(through, 'dp', [(i, i ^ (4 if i & 1 == 0 else 2)) for i in r...  4.34 us
  transfers between devices with their start and end apart: 26, of which 11 were waited for; matrix products, arithmetic and copies ran while one was open for 1% of the time, Pallas kernels for 25%

commit v1 on v0

--- a/solution.py
+++ b/solution.py
@@ -373,7 +373,7 @@
     o1 = move(up, *MIDDLE)
 
     gathered = gather_rows(own, d)
-    cut = 3 * hidden // 7 // 512 * 512
+    cut = (hidden // 512 + 1) // 2 * 512
     block = rows * len(gathered) // groups
     q, *first = project_first(gathered, weight, cut, (block, block, 2 * block))
     own_a, pair_a, beyond_a = first[0]
@@ -383,6 +383,7 @@
     own_b, pair_b, far_b, near_b = project(q, weight, cut, hidden - cut, (block,) * 4)
 
     inward_a = move(beyond_a, *INWARD)
+    inward_a, own_b = after([inward_a, own_b])
     inward_far = move(far_b, *INWARD)
     (inward_near,) = after([near_b], inward_a)
     inward_near = move(inward_near, *INWARD)
@@ -391,6 +392,7 @@
     e3 = move(o2, *OUTWARD)
     inward_far, o2, e2 = after([inward_far, o2, e2])
     across_far = move(total(far_b, inward_far), *MIDDLE)
+    across_a, e3 = after([across_a, e3])
     out_a = swap(total(pair_a, across_a[:block]), "tensor", 1)
 
     (late,) = after([q], inward_far)

time: 117 us -> 133 us (1.14)
  waiting for transfers between devices: 32 us -> 62.6 us
  starting transfers between devices: 50.1 us -> 34 us
  local copies, waits for them, and re-layouts: 1.72 us -> 3.31 us
    ppermute x10, waiting for transfers between devices: 12.3 us -> 31.1 us  [move(): return lax.ppermute(block, 'tensor', pairs)]
    ppermute x15, starting transfers between devices: 26.8 us -> 14.8 us  [swap(): lax.ppermute(block, axis, [(i, i ^ mask) for i in range(count) if i ^ mas...]
    ppermute x15, waiting for transfers between devices: 15.4 us -> 27.2 us  [swap(): lax.ppermute(block, axis, [(i, i ^ mask) for i in range(count) if i ^ mas...]
    ppermute x10, starting transfers between devices: 21.8 us -> 17.6 us  [move(): return lax.ppermute(block, 'tensor', pairs)]
    unnamed x6 -> x8, local copies, waits for them, and re-layouts: 1.72 us -> 3.31 us
    pallas_call x1, Pallas kernels: 6.03 us -> 7.44 us  [project_first(): pl.pallas_call(first_kernel, out_shape=[jax.ShapeDtypeStruct((tokens, dep...]
    pallas_call x1, Pallas kernels: 7.14 us -> 5.77 us  [project(): pl.pallas_call(project_kernel, out_shape=[jax.ShapeDtypeStruct((block, wi...]
  transfers between devices with their start and end apart: 26 -> 26, of which waited for: 11 -> 14; matrix products, arithmetic and copies ran while one was open for 1% -> 1% of each run, Pallas kernels for 25% -> 22%
where the time goes in v1:
time: 133 us; the launch traced here: 132 us
  waiting for transfers between devices  62.6 us (47%)
  starting transfers between devices  34 us (26%)
  Pallas kernels  29 us (22%)
  local copies, waits for them, and re-layouts  3.31 us (2%)
  other arithmetic  2.58 us (2%)
    ppermute x10, waiting for transfers between devices, move(): return lax.ppermute(block, 'tensor', pairs)  31.1 us
    ppermute x15, waiting for transfers between devices, swap(): lax.ppermute(block, axis, [(i, i ^ mask) for i in range(count) if i ^ mas...  27.2 us
    ppermute x10, starting transfers between devices, move(): return lax.ppermute(block, 'tensor', pairs)  17.6 us
    pallas_call x2, Pallas kernels, weight_gradient(): pl.pallas_call(functools.partial(grad_kernel, tile, start), out_shape=jax...  14.8 us
    ppermute x15, starting transfers between devices, swap(): lax.ppermute(block, axis, [(i, i ^ mask) for i in range(count) if i ^ mas...  14.8 us
    pallas_call x1, Pallas kernels, project_first(): pl.pallas_call(first_kernel, out_shape=[jax.ShapeDtypeStruct((tokens, dep...  7.44 us
    pallas_call x1, Pallas kernels, project(): pl.pallas_call(project_kernel, out_shape=[jax.ShapeDtypeStruct((block, wi...  5.77 us
    ppermute x1, waiting for transfers between devices, gather_rows(): lax.ppermute(through, 'dp', [(i, i ^ (4 if i & 1 == 0 else 2)) for i in r...  4.34 us
  transfers between devices with their start and end apart: 26, of which 14 were waited for; matrix products, arithmetic and copies ran while one was open for 1% of the time, Pallas kernels for 22%

profile of v1, /device:TPU:0, one launch (start us, length us, event | category | flops | bytes accessed | tf_op | source)
XLA Modules:
  0.0 132.4 jit_solution(630802107636110631)
XLA Ops:
  0.6 1.0 copy-done.2
  1.7 0.7 copy-done.3
  2.4 0.1 signed_pieces.1
  2.4 3.1 %collective-permute-start = (bf16[16,2048]{1,0:T(8,128)(2,1)S(1)}, bf16[16,2048]{1,0:T(8,128)(2,1)S(1)}, u32[]{:S(2)}, u32[]{:S(2)}) collective-permute-start(bf16[16,2048]{1,0:T(8,128)(2,1)S(1)} %get-tuple-element.43), channel_id=1, source_target_pairs={{0,1},{1,0},{2,3},{3,2},{4,5},{5,4},{6,7},{7,6},{8,9},{9,8},{10,11... | collective-permute-start | bytes 196616 | tf_op jit(solution)/shard_map/ppermute | solution.py:27
  5.5 2.6 %collective-permute-start.1 = (bf16[16,2048]{1,0:T(8,128)(2,1)S(1)}, bf16[16,2048]{1,0:T(8,128)(2,1)S(1)}, u32[]{:S(2)}, u32[]{:S(2)}) collective-permute-start(bf16[16,2048]{1,0:T(8,128)(2,1)S(1)} %get-tuple-element.44), channel_id=1, source_target_pairs={{0,2},{1,3},{2,0},{3,1},{4,6},{5,7},{6,4},{7,5},{8,10},{9,11},{10,... | collective-permute-start | bytes 196616 | tf_op jit(solution)/shard_map/ppermute | solution.py:27
  8.1 0.3 fusion.3.h_ref
  8.4 0.0 collective-permute-done.refs_1_
  8.5 4.3 %collective-permute-done.1.refs_2_ = bf16[16,2048]{1,0:T(8,128)(2,1)S(1)} collective-permute-done((bf16[16,2048]{1,0:T(8,128)(2,1)S(1)}, bf16[16,2048]{1,0:T(8,128)(2,1)S(1)}, u32[]{:S(2)}, u32[]{:S(2)}) %collective-permute-start.1) | collective-permute-done | bytes 65568 | tf_op jit(solution)/shard_map/ppermute | solution.py:27
  12.8 1.4 %collective-permute-done.2.refs_3_ = bf16[16,2048]{1,0:T(8,128)(2,1)S(1)} collective-permute-done((bf16[16,2048]{1,0:T(8,128)(2,1)S(1)}, bf16[16,2048]{1,0:T(8,128)(2,1)S(1)}, u32[]{:S(2)}, u32[]{:S(2)}) %collective-permute-start.2) | collective-permute-done | bytes 65568 | tf_op jit(solution)/shard_map/ppermute | solution.py:27
  14.2 0.3 rotate.1
  14.5 1.6 %collective-permute-start.4 = (bf16[16,2048]{1,0:T(8,128)(2,1)S(1)}, bf16[16,2048]{1,0:T(8,128)(2,1)S(1)}, u32[]{:S(2)}, u32[]{:S(2)}) collective-permute-start(bf16[16,2048]{1,0:T(8,128)(2,1)S(1)} %get-tuple-element.48), channel_id=1, source_target_pairs={{0,2},{1,3},{2,0},{3,1},{4,6},{5,7},{6,4},{7,5},{8,10},{9,11},{10,... | collective-permute-start | bytes 196616 | tf_op jit(solution)/shard_map/ppermute | solution.py:27
  16.1 0.7 collective-permute-start.5
  16.8 1.2 collective-permute-start.3
  18.0 2.4 %collective-permute-done.4 = bf16[16,2048]{1,0:T(8,128)(2,1)S(1)} collective-permute-done((bf16[16,2048]{1,0:T(8,128)(2,1)S(1)}, bf16[16,2048]{1,0:T(8,128)(2,1)S(1)}, u32[]{:S(2)}, u32[]{:S(2)}) %collective-permute-start.4) | collective-permute-done | bytes 65568 | tf_op jit(solution)/shard_map/ppermute | solution.py:27
  20.5 1.7 %collective-permute-done.5 = bf16[16,2048]{1,0:T(8,128)(2,1)S(1)} collective-permute-done((bf16[16,2048]{1,0:T(8,128)(2,1)S(1)}, bf16[16,2048]{1,0:T(8,128)(2,1)S(1)}, u32[]{:S(2)}, u32[]{:S(2)}) %collective-permute-start.5) | collective-permute-done | bytes 65568 | tf_op jit(solution)/shard_map/ppermute | solution.py:27
  22.2 0.0 collective-permute-done.3
  22.3 1.6 %collective-permute-start.7 = (bf16[64,2048]{1,0:T(8,128)(2,1)S(1)}, bf16[64,2048]{1,0:T(8,128)(2,1)S(1)}, u32[]{:S(2)}, u32[]{:S(2)}) collective-permute-start(bf16[64,2048]{1,0:T(8,128)(2,1)S(1)} %pad_maximum_fusion.1.refs_0_), channel_id=1, source_target_pairs={{0,8},{4,12},{8,0},{12,4},{16,24},{20,28},{24,16},{28,20},{1,9},{5... | collective-permute-start | bytes 786440 | tf_op jit(solution)/shard_map/ppermute | solution.py:27
  23.8 1.5 %collective-permute-start.8 = (bf16[64,2048]{1,0:T(8,128)(2,1)S(1)}, bf16[64,2048]{1,0:T(8,128)(2,1)S(1)}, u32[]{:S(2)}, u32[]{:S(2)}) collective-permute-start(bf16[64,2048]{1,0:T(8,128)(2,1)S(1)} %pad_maximum_fusion.1.refs_0_), channel_id=1, source_target_pairs={{0,16},{4,20},{8,24},{12,28},{16,0},{20,4},{24,8},{28,12},{1,17},{... | collective-permute-start | bytes 786440 | tf_op jit(solution)/shard_map/ppermute | solution.py:27
  25.4 3.4 %collective-permute-done.7.refs_2_ = bf16[64,2048]{1,0:T(8,128)(2,1)S(1)} collective-permute-done((bf16[64,2048]{1,0:T(8,128)(2,1)S(1)}, bf16[64,2048]{1,0:T(8,128)(2,1)S(1)}, u32[]{:S(2)}, u32[]{:S(2)}) %collective-permute-start.7) | collective-permute-done | bytes 262176 | tf_op jit(solution)/shard_map/ppermute | solution.py:27
  28.7 1.5 %collective-permute-done.8.refs_4_ = bf16[64,2048]{1,0:T(8,128)(2,1)S(1)} collective-permute-done((bf16[64,2048]{1,0:T(8,128)(2,1)S(1)}, bf16[64,2048]{1,0:T(8,128)(2,1)S(1)}, u32[]{:S(2)}, u32[]{:S(2)}) %collective-permute-start.8) | collective-permute-done | bytes 262176 | tf_op jit(solution)/shard_map/ppermute | solution.py:27
  30.2 1.6 %collective-permute-start.11 = (bf16[64,2048]{1,0:T(8,128)(2,1)S(1)}, bf16[64,2048]{1,0:T(8,128)(2,1)S(1)}, u32[]{:S(2)}, u32[]{:S(2)}) collective-permute-start(bf16[64,2048]{1,0:T(8,128)(2,1)S(1)} %broadcast_select_fusion), channel_id=1, source_target_pairs={{0,16},{4,12},{8,24},{12,4},{16,0},{20,28},{24,8},{28,20},{1,17},{... | collective-permute-start | bytes 786440 | tf_op jit(solution)/shard_map/ppermute | solution.py:162
  31.8 0.0 collective-permute-start.6
  31.8 0.5 collective-permute-start.9
  32.3 0.0 collective-permute-start.10
  32.3 4.3 %collective-permute-done.11.refs_6_ = bf16[64,2048]{1,0:T(8,128)(2,1)S(1)} collective-permute-done((bf16[64,2048]{1,0:T(8,128)(2,1)S(1)}, bf16[64,2048]{1,0:T(8,128)(2,1)S(1)}, u32[]{:S(2)}, u32[]{:S(2)}) %collective-permute-start.11) | collective-permute-done | bytes 262176 | tf_op jit(solution)/shard_map/ppermute | solution.py:162
  36.7 0.0 collective-permute-start.12
  36.7 0.1 collective-permute-start.13
  36.8 0.7 collective-permute-start.14
  37.5 0.0 collective-permute-done.9.refs_3_
  37.5 0.7 collective-permute-done.12.refs_7_
  38.2 7.4 %project_first.1 = (bf16[512,2048]{1,0:T(8,128)(2,1)}, bf16[128,2048]{1,0:T(8,128)(2,1)S(1)}, bf16[128,2048]{1,0:T(8,128)(2,1)S(1)}, bf16[256,2048]{1,0:T(8,128)(2,1)S(1)}) custom-call(bf16[64,2048]{1,0:T(8,128)(2,1)S(1)} %pad_maximum_fusion.1.refs_0_, bf16[64,2048]{1,0:T(8,128)(2,1)S(1)} %collective-permute-done.6.refs_1_, ...), custom_call_target="tpu_custom_call" | custom-call | flops 1 | bytes 1 | tf_op jit(solution)/shard_map/project_first/pallas_call | solution.py:221
  45.7 5.6 %collective-permute-start.18 = (bf16[256,2048]{1,0:T(8,128)(2,1)S(1)}, bf16[256,2048]{1,0:T(8,128)(2,1)S(1)}, u32[]{:S(2)}, u32[]{:S(2)}) collective-permute-start(bf16[256,2048]{1,0:T(8,128)(2,1)S(1)} %get-tuple-element.59), channel_id=1, source_target_pairs={{0,1},{3,2},{4,5},{7,6},{8,9},{11,10},{12,13},{15,14},{16,17},{19,... | collective-permute-start | bytes 3145736 | tf_op jit(solution)/shard_map/ppermute | solution.py:346
  51.2 8.2 %collective-permute-done.13.e1 = bf16[128,3584]{1,0:T(8,128)(2,1)S(1)} collective-permute-done((bf16[128,3584]{1,0:T(8,128)(2,1)S(1)}, bf16[128,3584]{1,0:T(8,128)(2,1)S(1)}, u32[]{:S(2)}, u32[]{:S(2)}) %collective-permute-start.13) | collective-permute-done | bytes 917536 | tf_op jit(solution)/shard_map/ppermute | solution.py:27
  59.4 0.7 collective-permute-start.16
  60.2 1.3 collective-permute-start.17
  61.5 0.0 copy-start
  61.5 1.6 %copy-done = bf16[512,2048]{1,0:T(8,128)(2,1)S(1)} copy-done((bf16[512,2048]{1,0:T(8,128)(2,1)S(1)}, bf16[512,2048]{1,0:T(8,128)(2,1)}, u32[]{:S(2)}) %copy-start) | copy-done | bytes 2097176
  63.1 5.8 %project.1 = (bf16[128,1536]{1,0:T(8,128)(2,1)S(1)}, bf16[128,1536]{1,0:T(8,128)(2,1)S(1)}, bf16[128,1536]{1,0:T(8,128)(2,1)S(1)}, bf16[128,1536]{1,0:T(8,128)(2,1)S(1)}) custom-call(bf16[512,2048]{1,0:T(8,128)(2,1)S(1)} %copy-done, bf16[2048,3584]{1,0:T(8,128)(2,1)} %w_ref.1), custom_call_target="tpu_custom_call" | custom-call | flops 3221225472 | bytes 9961472 | tf_op jit(solution)/shard_map/project/pallas_call | solution.py:243
  68.8 10.9 %collective-permute-done.18 = bf16[256,2048]{1,0:T(8,128)(2,1)S(1)} collective-permute-done((bf16[256,2048]{1,0:T(8,128)(2,1)S(1)}, bf16[256,2048]{1,0:T(8,128)(2,1)S(1)}, u32[]{:S(2)}, u32[]{:S(2)}) %collective-permute-start.18) | collective-permute-done | bytes 1048608 | tf_op jit(solution)/shard_map/ppermute | solution.py:346
  79.7 0.4 add_convert_fusion
  80.1 0.7 collective-permute-start.21
  80.8 0.0 collective-permute-done.16.o2
  80.9 6.2 %collective-permute-done.17.e2 = bf16[128,3584]{1,0:T(8,128)(2,1)S(1)} collective-permute-done((bf16[128,3584]{1,0:T(8,128)(2,1)S(1)}, bf16[128,3584]{1,0:T(8,128)(2,1)S(1)}, u32[]{:S(2)}, u32[]{:S(2)}) %collective-permute-start.17) | collective-permute-done | bytes 917536 | tf_op jit(solution)/shard_map/ppermute | solution.py:346
  87.0 1.3 collective-permute-start.22
  88.3 4.6 %collective-permute-start.15 = (bf16[128,1536]{1,0:T(8,128)(2,1)S(1)}, bf16[128,1536]{1,0:T(8,128)(2,1)S(1)}, u32[]{:S(2)}, u32[]{:S(2)}) collective-permute-start(bf16[128,1536]{1,0:T(8,128)(2,1)S(1)} %get-tuple-element.56), channel_id=1, source_target_pairs={{0,1},{3,2},{4,5},{7,6},{8,9},{11,10},{12,13},{15,14},{16,17},{19,... | collective-permute-start | bytes 1179656 | tf_op jit(solution)/shard_map/ppermute | solution.py:346
  92.9 1.3 collective-permute-start.20
  94.3 8.2 %collective-permute-done.15 = bf16[128,1536]{1,0:T(8,128)(2,1)S(1)} collective-permute-done((bf16[128,1536]{1,0:T(8,128)(2,1)S(1)}, bf16[128,1536]{1,0:T(8,128)(2,1)S(1)}, u32[]{:S(2)}, u32[]{:S(2)}) %collective-permute-start.15) | collective-permute-done | bytes 393248 | tf_op jit(solution)/shard_map/ppermute | solution.py:346
  102.5 0.6 transposed.1.q_t
  103.1 0.1 add_convert_fusion.6
  103.2 0.7 collective-permute-start.19
  103.9 5.8 %collective-permute-done.22.e3 = bf16[128,3584]{1,0:T(8,128)(2,1)S(1)} collective-permute-done((bf16[128,3584]{1,0:T(8,128)(2,1)S(1)}, bf16[128,3584]{1,0:T(8,128)(2,1)S(1)}, u32[]{:S(2)}, u32[]{:S(2)}) %collective-permute-start.22) | collective-permute-done | bytes 917536 | tf_op jit(solution)/shard_map/ppermute | solution.py:346
  109.6 0.1 add_convert_fusion.2
  109.8 0.9 collective-permute-start.23
  110.7 6.7 %weight_gradient.2.refs_0_ = f32[2048,3584]{1,0:T(8,128)} custom-call(bf16[2048,512]{1,0:T(8,128)(2,1)S(1)} %transposed.1.q_t, bf16[128,3584]{1,0:T(8,128)(2,1)S(1)} %copy-done.1, bf16[128,3584]{1,0:T(8,128)(2,1)S(1)} %collective-permute-done.13.e1, bf16[128,3584]{1,0:T(8,128)(2,1)S(1)} %collective-permute-done.14.o1, ...), custom_call_target="tpu_custom_call" | custom-call | flops 3221225472 | bytes 16252928 | tf_op jit(solution)/shard_map/weight_gradient/pallas_call | solution.py:320
  117.5 0.1 add_convert_fusion.4
  117.6 0.7 collective-permute-start.25
  118.2 0.0 collective-permute-done.19
  118.3 3.5 %collective-permute-done.23 = bf16[128,2048]{1,0:T(8,128)(2,1)S(1)} collective-permute-done((bf16[128,2048]{1,0:T(8,128)(2,1)S(1)}, bf16[128,2048]{1,0:T(8,128)(2,1)S(1)}, u32[]{:S(2)}, u32[]{:S(2)}) %collective-permute-start.23) | collective-permute-done | bytes 524320 | tf_op jit(solution)/shard_map/ppermute | solution.py:27
  121.8 0.1 add_convert_fusion.5
  121.9 0.9 collective-permute-start.24
  122.8 0.2 add_convert_fusion.1
  123.1 8.1 %weight_gradient.3 = f32[2048,3584]{1,0:T(8,128)} custom-call(bf16[2048,512]{1,0:T(8,128)(2,1)S(1)} %transposed.1.q_t, bf16[128,3584]{1,0:T(8,128)(2,1)S(1)} %copy-done.1, bf16[128,3584]{1,0:T(8,128)(2,1)S(1)} %collective-permute-done.13.e1, bf16[128,3584]{1,0:T(8,128)(2,1)S(1)} %collective-permute-done.14.o1, ...), custom_call_target="tpu_custom_call", output_to_operand_aliasing={{}: (7, {})} | custom-call | flops 4294967296 | bytes 20971520 | tf_op jit(solution)/shard_map/weight_gradient/pallas_call | solution.py:320
  131.2 0.1 add_convert_fusion.3
  131.4 1.0 pad_maximum_fusion
  (15 shorter events, 0.1 us)
Async XLA Ops:
  0.6 36.1 %copy-start.1 = (bf16[128,3584]{1,0:T(8,128)(2,1)S(1)}, bf16[128,3584]{1,0:T(8,128)(2,1)}, u32[]{:S(2)}) copy-start(bf16[128,3584]{1,0:T(8,128)(2,1)} %own_ref.3) | copy-start | bytes 2752516
  0.6 1.0 copy-start.2
  1.7 0.7 copy-start.3
  2.4 6.0 %collective-permute-start = (bf16[16,2048]{1,0:T(8,128)(2,1)S(1)}, bf16[16,2048]{1,0:T(8,128)(2,1)S(1)}, u32[]{:S(2)}, u32[]{:S(2)}) collective-permute-start(bf16[16,2048]{1,0:T(8,128)(2,1)S(1)} %get-tuple-element.43), channel_id=1, source_target_pairs={{0,1},{1,0},{2,3},{3,2},{4,5},{5,4},{6,7},{7,6},{8,9},{9,8},{10,11... | collective-permute-start | bytes 196616 | tf_op jit(solution)/shard_map/ppermute | solution.py:27
  5.5 7.3 %collective-permute-start.1 = (bf16[16,2048]{1,0:T(8,128)(2,1)S(1)}, bf16[16,2048]{1,0:T(8,128)(2,1)S(1)}, u32[]{:S(2)}, u32[]{:S(2)}) collective-permute-start(bf16[16,2048]{1,0:T(8,128)(2,1)S(1)} %get-tuple-element.44), channel_id=1, source_target_pairs={{0,2},{1,3},{2,0},{3,1},{4,6},{5,7},{6,4},{7,5},{8,10},{9,11},{10,... | collective-permute-start | bytes 196616 | tf_op jit(solution)/shard_map/ppermute | solution.py:27
  8.1 6.1 %collective-permute-start.2 = (bf16[16,2048]{1,0:T(8,128)(2,1)S(1)}, bf16[16,2048]{1,0:T(8,128)(2,1)S(1)}, u32[]{:S(2)}, u32[]{:S(2)}) collective-permute-start(bf16[16,2048]{1,0:T(8,128)(2,1)S(1)} %get-tuple-element.45), channel_id=1, source_target_pairs={{0,3},{1,2},{2,1},{3,0},{4,7},{5,6},{6,5},{7,4},{8,11},{9,10},{10,... | collective-permute-start | bytes 196616 | tf_op jit(solution)/shard_map/ppermute | solution.py:27
  14.5 6.0 %collective-permute-start.4 = (bf16[16,2048]{1,0:T(8,128)(2,1)S(1)}, bf16[16,2048]{1,0:T(8,128)(2,1)S(1)}, u32[]{:S(2)}, u32[]{:S(2)}) collective-permute-start(bf16[16,2048]{1,0:T(8,128)(2,1)S(1)} %get-tuple-element.48), channel_id=1, source_target_pairs={{0,2},{1,3},{2,0},{3,1},{4,6},{5,7},{6,4},{7,5},{8,10},{9,11},{10,... | collective-permute-start | bytes 196616 | tf_op jit(solution)/shard_map/ppermute | solution.py:27
  16.1 6.1 %collective-permute-start.5 = (bf16[16,2048]{1,0:T(8,128)(2,1)S(1)}, bf16[16,2048]{1,0:T(8,128)(2,1)S(1)}, u32[]{:S(2)}, u32[]{:S(2)}) collective-permute-start(bf16[16,2048]{1,0:T(8,128)(2,1)S(1)} %get-tuple-element.49), channel_id=1, source_target_pairs={{0,3},{1,2},{2,1},{3,0},{4,7},{5,6},{6,5},{7,4},{8,11},{9,10},{10,... | collective-permute-start | bytes 196616 | tf_op jit(solution)/shard_map/ppermute | solution.py:27
  16.8 5.4 %collective-permute-start.3 = (bf16[16,2048]{1,0:T(8,128)(2,1)S(1)}, bf16[16,2048]{1,0:T(8,128)(2,1)S(1)}, u32[]{:S(2)}, u32[]{:S(2)}) collective-permute-start(bf16[16,2048]{1,0:T(8,128)(2,1)S(1)} %get-tuple-element.47), channel_id=1, source_target_pairs={{0,1},{1,0},{2,3},{3,2},{4,5},{5,4},{6,7},{7,6},{8,9},{9,8},{10,11... | collective-permute-start | bytes 196616 | tf_op jit(solution)/shard_map/ppermute | solution.py:27
  22.3 6.4 %collective-permute-start.7 = (bf16[64,2048]{1,0:T(8,128)(2,1)S(1)}, bf16[64,2048]{1,0:T(8,128)(2,1)S(1)}, u32[]{:S(2)}, u32[]{:S(2)}) collective-permute-start(bf16[64,2048]{1,0:T(8,128)(2,1)S(1)} %pad_maximum_fusion.1.refs_0_), channel_id=1, source_target_pairs={{0,8},{4,12},{8,0},{12,4},{16,24},{20,28},{24,16},{28,20},{1,9},{5... | collective-permute-start | bytes 786440 | tf_op jit(solution)/shard_map/ppermute | solution.py:27
  23.8 6.4 %collective-permute-start.8 = (bf16[64,2048]{1,0:T(8,128)(2,1)S(1)}, bf16[64,2048]{1,0:T(8,128)(2,1)S(1)}, u32[]{:S(2)}, u32[]{:S(2)}) collective-permute-start(bf16[64,2048]{1,0:T(8,128)(2,1)S(1)} %pad_maximum_fusion.1.refs_0_), channel_id=1, source_target_pairs={{0,16},{4,20},{8,24},{12,28},{16,0},{20,4},{24,8},{28,12},{1,17},{... | collective-permute-start | bytes 786440 | tf_op jit(solution)/shard_map/ppermute | solution.py:27
  30.2 6.4 %collective-permute-start.11 = (bf16[64,2048]{1,0:T(8,128)(2,1)S(1)}, bf16[64,2048]{1,0:T(8,128)(2,1)S(1)}, u32[]{:S(2)}, u32[]{:S(2)}) collective-permute-start(bf16[64,2048]{1,0:T(8,128)(2,1)S(1)} %broadcast_select_fusion), channel_id=1, source_target_pairs={{0,16},{4,12},{8,24},{12,4},{16,0},{20,28},{24,8},{28,20},{1,17},{... | collective-permute-start | bytes 786440 | tf_op jit(solution)/shard_map/ppermute | solution.py:162
  31.8 5.0 %collective-permute-start.6 = (bf16[64,2048]{1,0:T(8,128)(2,1)S(1)}, bf16[64,2048]{1,0:T(8,128)(2,1)S(1)}, u32[]{:S(2)}, u32[]{:S(2)}) collective-permute-start(bf16[64,2048]{1,0:T(8,128)(2,1)S(1)} %pad_maximum_fusion.1.refs_0_), channel_id=1, source_target_pairs={{0,4},{4,0},{8,12},{12,8},{16,20},{20,16},{24,28},{28,24},{1,5},{5... | collective-permute-start | bytes 786440 | tf_op jit(solution)/shard_map/ppermute | solution.py:27
  31.8 5.7 %collective-permute-start.9 = (bf16[64,2048]{1,0:T(8,128)(2,1)S(1)}, bf16[64,2048]{1,0:T(8,128)(2,1)S(1)}, u32[]{:S(2)}, u32[]{:S(2)}) collective-permute-start(bf16[64,2048]{1,0:T(8,128)(2,1)S(1)} %collective-permute-done.7.refs_2_), channel_id=1, source_target_pairs={{0,4},{4,0},{8,12},{12,8},{16,20},{20,16},{24,28},{28,24},{1,5},{5... | collective-permute-start | bytes 786440 | tf_op jit(solution)/shard_map/ppermute | solution.py:27
  32.3 5.2 %collective-permute-start.10 = (bf16[64,2048]{1,0:T(8,128)(2,1)S(1)}, bf16[64,2048]{1,0:T(8,128)(2,1)S(1)}, u32[]{:S(2)}, u32[]{:S(2)}) collective-permute-start(bf16[64,2048]{1,0:T(8,128)(2,1)S(1)} %collective-permute-done.8.refs_4_), channel_id=1, source_target_pairs={{0,4},{4,0},{8,12},{12,8},{16,20},{20,16},{24,28},{28,24},{1,5},{5... | collective-permute-start | bytes 786440 | tf_op jit(solution)/shard_map/ppermute | solution.py:27
  36.7 1.5 %collective-permute-start.12 = (bf16[64,2048]{1,0:T(8,128)(2,1)S(1)}, bf16[64,2048]{1,0:T(8,128)(2,1)S(1)}, u32[]{:S(2)}, u32[]{:S(2)}) collective-permute-start(bf16[64,2048]{1,0:T(8,128)(2,1)S(1)} %collective-permute-done.11.refs_6_), channel_id=1, source_target_pairs={{0,4},{4,0},{8,12},{12,8},{16,20},{20,16},{24,28},{28,24},{1,5},{5... | collective-permute-start | bytes 786440 | tf_op jit(solution)/shard_map/ppermute | solution.py:27
  36.7 22.8 %collective-permute-start.13 = (bf16[128,3584]{1,0:T(8,128)(2,1)S(1)}, bf16[128,3584]{1,0:T(8,128)(2,1)S(1)}, u32[]{:S(2)}, u32[]{:S(2)}) collective-permute-start(bf16[128,3584]{1,0:T(8,128)(2,1)S(1)} %copy-done.1), channel_id=1, source_target_pairs={{0,1},{1,0},{2,3},{3,2},{4,5},{5,4},{6,7},{7,6},{8,9},{9,8},{10,11... | collective-permute-start | bytes 2752520 | tf_op jit(solution)/shard_map/ppermute | solution.py:27
  36.8 22.7 %collective-permute-start.14 = (bf16[128,3584]{1,0:T(8,128)(2,1)S(1)}, bf16[128,3584]{1,0:T(8,128)(2,1)S(1)}, u32[]{:S(2)}, u32[]{:S(2)}) collective-permute-start(bf16[128,3584]{1,0:T(8,128)(2,1)S(1)} %copy-done.1), channel_id=1, source_target_pairs={{1,2},{2,1},{5,6},{6,5},{9,10},{10,9},{13,14},{14,13},{17,18},{18,... | collective-permute-start | bytes 2752520 | tf_op jit(solution)/shard_map/ppermute | solution.py:346
  45.7 34.1 %collective-permute-start.18 = (bf16[256,2048]{1,0:T(8,128)(2,1)S(1)}, bf16[256,2048]{1,0:T(8,128)(2,1)S(1)}, u32[]{:S(2)}, u32[]{:S(2)}) collective-permute-start(bf16[256,2048]{1,0:T(8,128)(2,1)S(1)} %get-tuple-element.59), channel_id=1, source_target_pairs={{0,1},{3,2},{4,5},{7,6},{8,9},{11,10},{12,13},{15,14},{16,17},{19,... | collective-permute-start | bytes 3145736 | tf_op jit(solution)/shard_map/ppermute | solution.py:346
  59.4 21.4 %collective-permute-start.16 = (bf16[128,3584]{1,0:T(8,128)(2,1)S(1)}, bf16[128,3584]{1,0:T(8,128)(2,1)S(1)}, u32[]{:S(2)}, u32[]{:S(2)}) collective-permute-start(bf16[128,3584]{1,0:T(8,128)(2,1)S(1)} %collective-permute-done.13.e1), channel_id=1, source_target_pairs={{1,2},{2,1},{5,6},{6,5},{9,10},{10,9},{13,14},{14,13},{17,18},{18,... | collective-permute-start | bytes 2752520 | tf_op jit(solution)/shard_map/ppermute | solution.py:346
  60.2 26.9 %collective-permute-start.17 = (bf16[128,3584]{1,0:T(8,128)(2,1)S(1)}, bf16[128,3584]{1,0:T(8,128)(2,1)S(1)}, u32[]{:S(2)}, u32[]{:S(2)}) collective-permute-start(bf16[128,3584]{1,0:T(8,128)(2,1)S(1)} %collective-permute-done.14.o1), channel_id=1, source_target_pairs={{1,0},{2,3},{5,4},{6,7},{9,8},{10,11},{13,12},{14,15},{17,16},{18,... | collective-permute-start | bytes 2752520 | tf_op jit(solution)/shard_map/ppermute | solution.py:346
  61.5 1.6 %copy-start = (bf16[512,2048]{1,0:T(8,128)(2,1)S(1)}, bf16[512,2048]{1,0:T(8,128)(2,1)}, u32[]{:S(2)}) copy-start(bf16[512,2048]{1,0:T(8,128)(2,1)} %get-tuple-element.67.q_ref) | copy-start | bytes 6291460
  80.1 29.5 %collective-permute-start.21 = (bf16[256,2048]{1,0:T(8,128)(2,1)S(1)}, bf16[256,2048]{1,0:T(8,128)(2,1)S(1)}, u32[]{:S(2)}, u32[]{:S(2)}) collective-permute-start(bf16[256,2048]{1,0:T(8,128)(2,1)S(1)} %add_convert_fusion), channel_id=1, source_target_pairs={{1,2},{2,1},{5,6},{6,5},{9,10},{10,9},{13,14},{14,13},{17,18},{18,... | collective-permute-start | bytes 3145736 | tf_op jit(solution)/shard_map/ppermute | solution.py:346
  87.0 22.6 %collective-permute-start.22 = (bf16[128,3584]{1,0:T(8,128)(2,1)S(1)}, bf16[128,3584]{1,0:T(8,128)(2,1)S(1)}, u32[]{:S(2)}, u32[]{:S(2)}) collective-permute-start(bf16[128,3584]{1,0:T(8,128)(2,1)S(1)} %collective-permute-done.16.o2), channel_id=1, source_target_pairs={{1,0},{2,3},{5,4},{6,7},{9,8},{10,11},{13,12},{14,15},{17,16},{18,... | collective-permute-start | bytes 2752520 | tf_op jit(solution)/shard_map/ppermute | solution.py:346
  88.3 14.2 %collective-permute-start.15 = (bf16[128,1536]{1,0:T(8,128)(2,1)S(1)}, bf16[128,1536]{1,0:T(8,128)(2,1)S(1)}, u32[]{:S(2)}, u32[]{:S(2)}) collective-permute-start(bf16[128,1536]{1,0:T(8,128)(2,1)S(1)} %get-tuple-element.56), channel_id=1, source_target_pairs={{0,1},{3,2},{4,5},{7,6},{8,9},{11,10},{12,13},{15,14},{16,17},{19,... | collective-permute-start | bytes 1179656 | tf_op jit(solution)/shard_map/ppermute | solution.py:346
  92.9 24.5 %collective-permute-start.20 = (bf16[128,1536]{1,0:T(8,128)(2,1)S(1)}, bf16[128,1536]{1,0:T(8,128)(2,1)S(1)}, u32[]{:S(2)}, u32[]{:S(2)}) collective-permute-start(bf16[128,1536]{1,0:T(8,128)(2,1)S(1)} %get-tuple-element.66), channel_id=1, source_target_pairs={{0,1},{3,2},{4,5},{7,6},{8,9},{11,10},{12,13},{15,14},{16,17},{19,... | collective-permute-start | bytes 1179656 | tf_op jit(solution)/shard_map/ppermute | solution.py:346
  103.2 15.1 %collective-permute-start.19 = (bf16[128,1536]{1,0:T(8,128)(2,1)S(1)}, bf16[128,1536]{1,0:T(8,128)(2,1)S(1)}, u32[]{:S(2)}, u32[]{:S(2)}) collective-permute-start(bf16[128,1536]{1,0:T(8,128)(2,1)S(1)} %add_convert_fusion.6), channel_id=1, source_target_pairs={{1,2},{2,1},{5,6},{6,5},{9,10},{10,9},{13,14},{14,13},{17,18},{18,... | collective-permute-start | bytes 1179656 | tf_op jit(solution)/shard_map/ppermute | solution.py:346
  109.8 12.0 %collective-permute-start.23 = (bf16[128,2048]{1,0:T(8,128)(2,1)S(1)}, bf16[128,2048]{1,0:T(8,128)(2,1)S(1)}, u32[]{:S(2)}, u32[]{:S(2)}) collective-permute-start(bf16[128,2048]{1,0:T(8,128)(2,1)S(1)} %add_convert_fusion.2), channel_id=1, source_target_pairs={{0,1},{1,0},{2,3},{3,2},{4,5},{5,4},{6,7},{7,6},{8,9},{9,8},{10,11... | collective-permute-start | bytes 1572872 | tf_op jit(solution)/shard_map/ppermute | solution.py:27
  117.6 13.7 %collective-permute-start.25 = (bf16[128,1536]{1,0:T(8,128)(2,1)S(1)}, bf16[128,1536]{1,0:T(8,128)(2,1)S(1)}, u32[]{:S(2)}, u32[]{:S(2)}) collective-permute-start(bf16[128,1536]{1,0:T(8,128)(2,1)S(1)} %add_convert_fusion.4), channel_id=1, source_target_pairs={{1,2},{2,1},{5,6},{6,5},{9,10},{10,9},{13,14},{14,13},{17,18},{18,... | collective-permute-start | bytes 1179656 | tf_op jit(solution)/shard_map/ppermute | solution.py:346
  121.9 9.4 %collective-permute-start.24 = (bf16[128,1536]{1,0:T(8,128)(2,1)S(1)}, bf16[128,1536]{1,0:T(8,128)(2,1)S(1)}, u32[]{:S(2)}, u32[]{:S(2)}) collective-permute-start(bf16[128,1536]{1,0:T(8,128)(2,1)S(1)} %add_convert_fusion.5), channel_id=1, source_target_pairs={{0,1},{1,0},{2,3},{3,2},{4,5},{5,4},{6,7},{7,6},{8,9},{9,8},{10,11... | collective-permute-start | bytes 1179656 | tf_op jit(solution)/shard_map/ppermute | solution.py:27

commit v2 on v0

--- a/solution.py
+++ b/solution.py
@@ -380,28 +380,23 @@
     q, e1, o1 = after([q, e1, o1])
     o2 = move(e1, *MIDDLE)
     e2 = move(o1, *OUTWARD)
-    own_b, pair_b, far_b, near_b = project(q, weight, cut, hidden - cut, (block,) * 4)
+    own_b, pair_b, beyond_b = project(q, weight, cut, hidden - cut, (block, block, 2 * block))
 
     inward_a = move(beyond_a, *INWARD)
-    inward_far = move(far_b, *INWARD)
-    (inward_near,) = after([near_b], inward_a)
-    inward_near = move(inward_near, *INWARD)
+    inward_b = move(beyond_b, *INWARD)
+    inward_a, o2, e2 = after([inward_a, o2, e2])
     across_a = move(total(beyond_a, inward_a), *MIDDLE)
-    o2, e2 = after([o2, e2], inward_a)
     e3 = move(o2, *OUTWARD)
-    inward_far, o2, e2 = after([inward_far, o2, e2])
-    across_far = move(total(far_b, inward_far), *MIDDLE)
+    across_far = move(total(beyond_b[:block], inward_b[:block]), *MIDDLE)
+    across_near = move(total(beyond_b[block:], inward_b[block:]), *MIDDLE)
+    across_a, e3 = after([across_a, e3])
     out_a = swap(total(pair_a, across_a[:block]), "tensor", 1)
 
-    (late,) = after([q], inward_far)
-    q_t = transposed(late)
+    q_t = transposed(after([q], inward_a)[0])
     moved = (e1, o1, o2, e2, e3)
     some = hidden // 2 // 512 * 512
     (late,) = after([q_t], across_a)
     grad = weight_gradient(late, upstream, moved, 0, some)
-
-    inward_near, grad = after([inward_near, grad])
-    across_near = move(total(near_b, inward_near), *MIDDLE)
     across_far, grad, out_a = after([across_far, grad, out_a])
     out_b = swap(total(pair_b, across_far), "tensor", 1)
     (late,) = after([q_t], across_far)

time: 117 us -> 120 us (1.026)
  waiting for transfers between devices: 32 us -> 44.9 us
  starting transfers between devices: 50.1 us -> 40.8 us
    ppermute x10 -> x9, waiting for transfers between devices: 12.3 us -> 25 us  [move(): return lax.ppermute(block, 'tensor', pairs)]
    ppermute x10 -> x9, starting transfers between devices: 21.8 us -> 15.8 us  [move(): return lax.ppermute(block, 'tensor', pairs)]
    ppermute x15, starting transfers between devices: 26.8 us -> 23.4 us  [swap(): lax.ppermute(block, axis, [(i, i ^ mask) for i in range(count) if i ^ mas...]
  transfers between devices with their start and end apart: 26 -> 25, of which waited for: 11 -> 11; matrix products, arithmetic and copies ran while one was open for 1% -> 1% of each run, Pallas kernels for 25% -> 24%
where the time goes in v2:
time: 120 us
  waiting for transfers between devices  44.9 us (37%)
  starting transfers between devices  40.8 us (34%)
  Pallas kernels  29 us (24%)
  other arithmetic  2.58 us (2%)
  local copies, waits for them, and re-layouts  1.72 us (1%)
    ppermute x9, waiting for transfers between devices, move(): return lax.ppermute(block, 'tensor', pairs)  25 us
    ppermute x15, starting transfers between devices, swap(): lax.ppermute(block, axis, [(i, i ^ mask) for i in range(count) if i ^ mas...  23.4 us
    ppermute x9, starting transfers between devices, move(): return lax.ppermute(block, 'tensor', pairs)  15.8 us
    ppermute x15, waiting for transfers between devices, swap(): lax.ppermute(block, axis, [(i, i ^ mask) for i in range(count) if i ^ mas...  15.6 us
    pallas_call x2, Pallas kernels, weight_gradient(): pl.pallas_call(functools.partial(grad_kernel, tile, start), out_shape=jax...  14.8 us
    pallas_call x1, Pallas kernels, project(): pl.pallas_call(project_kernel, out_shape=[jax.ShapeDtypeStruct((block, wi...  7.14 us
    pallas_call x1, Pallas kernels, project_first(): pl.pallas_call(first_kernel, out_shape=[jax.ShapeDtypeStruct((tokens, dep...  6.03 us
    ppermute x1, waiting for transfers between devices, gather_rows(): lax.ppermute(through, 'dp', [(i, i ^ (4 if i & 1 == 0 else 2)) for i in r...  4.34 us
  transfers between devices with their start and end apart: 25, of which 11 were waited for; matrix products, arithmetic and copies ran while one was open for 1% of the time, Pallas kernels for 24%

profile of v2, /device:TPU:0, one launch (start us, length us, event | category | flops | bytes accessed | tf_op | source)
XLA Modules:
  0.0 119.9 jit_solution(9551986360236000252)
XLA Ops:
  0.6 1.0 copy-done.1
  1.7 0.7 copy-done.2
  2.4 0.1 signed_pieces.1
  2.4 3.1 %collective-permute-start = (bf16[16,2048]{1,0:T(8,128)(2,1)S(1)}, bf16[16,2048]{1,0:T(8,128)(2,1)S(1)}, u32[]{:S(2)}, u32[]{:S(2)}) collective-permute-start(bf16[16,2048]{1,0:T(8,128)(2,1)S(1)} %get-tuple-element.35), channel_id=1, source_target_pairs={{0,1},{1,0},{2,3},{3,2},{4,5},{5,4},{6,7},{7,6},{8,9},{9,8},{10,11... | collective-permute-start | bytes 196616 | tf_op jit(solution)/shard_map/ppermute | solution.py:27
  5.5 2.6 %collective-permute-start.1 = (bf16[16,2048]{1,0:T(8,128)(2,1)S(1)}, bf16[16,2048]{1,0:T(8,128)(2,1)S(1)}, u32[]{:S(2)}, u32[]{:S(2)}) collective-permute-start(bf16[16,2048]{1,0:T(8,128)(2,1)S(1)} %get-tuple-element.36), channel_id=1, source_target_pairs={{0,2},{1,3},{2,0},{3,1},{4,6},{5,7},{6,4},{7,5},{8,10},{9,11},{10,... | collective-permute-start | bytes 196616 | tf_op jit(solution)/shard_map/ppermute | solution.py:27
  8.1 0.0 collective-permute-start.2
  8.1 0.3 fusion.3.h_ref
  8.4 0.0 collective-permute-done.refs_1_
  8.5 4.3 %collective-permute-done.1.refs_2_ = bf16[16,2048]{1,0:T(8,128)(2,1)S(1)} collective-permute-done((bf16[16,2048]{1,0:T(8,128)(2,1)S(1)}, bf16[16,2048]{1,0:T(8,128)(2,1)S(1)}, u32[]{:S(2)}, u32[]{:S(2)}) %collective-permute-start.1) | collective-permute-done | bytes 65568 | tf_op jit(solution)/shard_map/ppermute | solution.py:27
  12.8 1.4 %collective-permute-done.2.refs_3_ = bf16[16,2048]{1,0:T(8,128)(2,1)S(1)} collective-permute-done((bf16[16,2048]{1,0:T(8,128)(2,1)S(1)}, bf16[16,2048]{1,0:T(8,128)(2,1)S(1)}, u32[]{:S(2)}, u32[]{:S(2)}) %collective-permute-start.2) | collective-permute-done | bytes 65568 | tf_op jit(solution)/shard_map/ppermute | solution.py:27
  14.2 0.3 rotate.1
  14.5 1.6 %collective-permute-start.4 = (bf16[16,2048]{1,0:T(8,128)(2,1)S(1)}, bf16[16,2048]{1,0:T(8,128)(2,1)S(1)}, u32[]{:S(2)}, u32[]{:S(2)}) collective-permute-start(bf16[16,2048]{1,0:T(8,128)(2,1)S(1)} %get-tuple-element.40), channel_id=1, source_target_pairs={{0,2},{1,3},{2,0},{3,1},{4,6},{5,7},{6,4},{7,5},{8,10},{9,11},{10,... | collective-permute-start | bytes 196616 | tf_op jit(solution)/shard_map/ppermute | solution.py:27
  16.1 0.7 collective-permute-start.5
  16.8 1.2 %collective-permute-start.3 = (bf16[16,2048]{1,0:T(8,128)(2,1)S(1)}, bf16[16,2048]{1,0:T(8,128)(2,1)S(1)}, u32[]{:S(2)}, u32[]{:S(2)}) collective-permute-start(bf16[16,2048]{1,0:T(8,128)(2,1)S(1)} %get-tuple-element.39), channel_id=1, source_target_pairs={{0,1},{1,0},{2,3},{3,2},{4,5},{5,4},{6,7},{7,6},{8,9},{9,8},{10,11... | collective-permute-start | bytes 196616 | tf_op jit(solution)/shard_map/ppermute | solution.py:27
  18.0 2.4 %collective-permute-done.4 = bf16[16,2048]{1,0:T(8,128)(2,1)S(1)} collective-permute-done((bf16[16,2048]{1,0:T(8,128)(2,1)S(1)}, bf16[16,2048]{1,0:T(8,128)(2,1)S(1)}, u32[]{:S(2)}, u32[]{:S(2)}) %collective-permute-start.4) | collective-permute-done | bytes 65568 | tf_op jit(solution)/shard_map/ppermute | solution.py:27
  20.5 1.7 %collective-permute-done.5 = bf16[16,2048]{1,0:T(8,128)(2,1)S(1)} collective-permute-done((bf16[16,2048]{1,0:T(8,128)(2,1)S(1)}, bf16[16,2048]{1,0:T(8,128)(2,1)S(1)}, u32[]{:S(2)}, u32[]{:S(2)}) %collective-permute-start.5) | collective-permute-done | bytes 65568 | tf_op jit(solution)/shard_map/ppermute | solution.py:27
  22.2 0.0 collective-permute-done.3
  22.3 1.6 %collective-permute-start.7 = (bf16[64,2048]{1,0:T(8,128)(2,1)S(1)}, bf16[64,2048]{1,0:T(8,128)(2,1)S(1)}, u32[]{:S(2)}, u32[]{:S(2)}) collective-permute-start(bf16[64,2048]{1,0:T(8,128)(2,1)S(1)} %pad_maximum_fusion.1.refs_0_), channel_id=1, source_target_pairs={{0,8},{4,12},{8,0},{12,4},{16,24},{20,28},{24,16},{28,20},{1,9},{5... | collective-permute-start | bytes 786440 | tf_op jit(solution)/shard_map/ppermute | solution.py:27
  23.8 1.5 %collective-permute-start.8 = (bf16[64,2048]{1,0:T(8,128)(2,1)S(1)}, bf16[64,2048]{1,0:T(8,128)(2,1)S(1)}, u32[]{:S(2)}, u32[]{:S(2)}) collective-permute-start(bf16[64,2048]{1,0:T(8,128)(2,1)S(1)} %pad_maximum_fusion.1.refs_0_), channel_id=1, source_target_pairs={{0,16},{4,20},{8,24},{12,28},{16,0},{20,4},{24,8},{28,12},{1,17},{... | collective-permute-start | bytes 786440 | tf_op jit(solution)/shard_map/ppermute | solution.py:27
  25.4 0.1 collective-permute-start.13
  25.5 0.7 collective-permute-start.14
  26.2 0.1 collective-permute-start.6
  26.3 2.5 %collective-permute-done.7.refs_2_ = bf16[64,2048]{1,0:T(8,128)(2,1)S(1)} collective-permute-done((bf16[64,2048]{1,0:T(8,128)(2,1)S(1)}, bf16[64,2048]{1,0:T(8,128)(2,1)S(1)}, u32[]{:S(2)}, u32[]{:S(2)}) %collective-permute-start.7) | collective-permute-done | bytes 262176 | tf_op jit(solution)/shard_map/ppermute | solution.py:27
  28.7 1.5 %collective-permute-done.8.refs_4_ = bf16[64,2048]{1,0:T(8,128)(2,1)S(1)} collective-permute-done((bf16[64,2048]{1,0:T(8,128)(2,1)S(1)}, bf16[64,2048]{1,0:T(8,128)(2,1)S(1)}, u32[]{:S(2)}, u32[]{:S(2)}) %collective-permute-start.8) | collective-permute-done | bytes 262176 | tf_op jit(solution)/shard_map/ppermute | solution.py:27
  30.2 1.6 %collective-permute-start.11 = (bf16[64,2048]{1,0:T(8,128)(2,1)S(1)}, bf16[64,2048]{1,0:T(8,128)(2,1)S(1)}, u32[]{:S(2)}, u32[]{:S(2)}) collective-permute-start(bf16[64,2048]{1,0:T(8,128)(2,1)S(1)} %broadcast_select_fusion), channel_id=1, source_target_pairs={{0,16},{4,12},{8,24},{12,4},{16,0},{20,28},{24,8},{28,20},{1,17},{... | collective-permute-start | bytes 786440 | tf_op jit(solution)/shard_map/ppermute | solution.py:162
  31.8 0.0 collective-permute-start.9
  31.8 0.0 collective-permute-done.6.refs_1_
  31.8 0.5 collective-permute-start.10
  32.3 4.3 %collective-permute-done.11.refs_6_ = bf16[64,2048]{1,0:T(8,128)(2,1)S(1)} collective-permute-done((bf16[64,2048]{1,0:T(8,128)(2,1)S(1)}, bf16[64,2048]{1,0:T(8,128)(2,1)S(1)}, u32[]{:S(2)}, u32[]{:S(2)}) %collective-permute-start.11) | collective-permute-done | bytes 262176 | tf_op jit(solution)/shard_map/ppermute | solution.py:162
  36.7 0.0 collective-permute-start.12
  36.7 0.0 collective-permute-done.9.refs_3_
  36.7 0.0 collective-permute-done.10.refs_5_
  36.7 1.5 %collective-permute-done.12.refs_7_ = bf16[64,2048]{1,0:T(8,128)(2,1)S(1)} collective-permute-done((bf16[64,2048]{1,0:T(8,128)(2,1)S(1)}, bf16[64,2048]{1,0:T(8,128)(2,1)S(1)}, u32[]{:S(2)}, u32[]{:S(2)}) %collective-permute-start.12) | collective-permute-done | bytes 262176 | tf_op jit(solution)/shard_map/ppermute | solution.py:27
  38.2 6.0 %project_first.1 = (bf16[512,2048]{1,0:T(8,128)(2,1)S(1)}, bf16[128,1536]{1,0:T(8,128)(2,1)S(1)}, bf16[128,1536]{1,0:T(8,128)(2,1)S(1)}, bf16[256,1536]{1,0:T(8,128)(2,1)S(1)}) custom-call(bf16[64,2048]{1,0:T(8,128)(2,1)S(1)} %pad_maximum_fusion.1.refs_0_, bf16[64,2048]{1,0:T(8,128)(2,1)S(1)} %collective-permute-done.6.refs_1_, ...), custom_call_target="tpu_custom_call" | custom-call | flops 1 | bytes 1 | tf_op jit(solution)/shard_map/project_first/pallas_call | solution.py:221
  44.2 0.3 collective-permute-done.13.e1
  44.5 0.0 collective-permute-done.14.o1
  44.5 0.7 collective-permute-start.18
  45.2 1.3 %collective-permute-start.19 = (bf16[128,3584]{1,0:T(8,128)(2,1)S(1)}, bf16[128,3584]{1,0:T(8,128)(2,1)S(1)}, u32[]{:S(2)}, u32[]{:S(2)}) collective-permute-start(bf16[128,3584]{1,0:T(8,128)(2,1)S(1)} %collective-permute-done.14.o1), channel_id=1, source_target_pairs={{1,0},{2,3},{5,4},{6,7},{9,8},{10,11},{13,12},{14,15},{17,16},{18,... | collective-permute-start | bytes 2752520 | tf_op jit(solution)/shard_map/ppermute | solution.py:346
  46.5 8.3 %collective-permute-start.17 = (bf16[256,1536]{1,0:T(8,128)(2,1)S(1)}, bf16[256,1536]{1,0:T(8,128)(2,1)S(1)}, u32[]{:S(2)}, u32[]{:S(2)}) collective-permute-start(bf16[256,1536]{1,0:T(8,128)(2,1)S(1)} %get-tuple-element.49), channel_id=1, source_target_pairs={{0,1},{3,2},{4,5},{7,6},{8,9},{11,10},{12,13},{15,14},{16,17},{19,... | collective-permute-start | bytes 2359304 | tf_op jit(solution)/shard_map/ppermute | solution.py:346
  54.9 7.1 %project.1 = (bf16[128,2048]{1,0:T(8,128)(2,1)S(1)}, bf16[128,2048]{1,0:T(8,128)(2,1)S(1)}, bf16[256,2048]{1,0:T(8,128)(2,1)S(1)}) custom-call(bf16[512,2048]{1,0:T(8,128)(2,1)S(1)} %get-tuple-element.53.q_ref, bf16[2048,3584]{1,0:T(8,128)(2,1)} %w_ref.1), custom_call_target="tpu_custom_call" | custom-call | flops 4294967296 | bytes 12582912 | tf_op jit(solution)/shard_map/project/pallas_call | solution.py:243
  62.0 1.4 %collective-permute-start.15 = (bf16[256,2048]{1,0:T(8,128)(2,1)S(1)}, bf16[256,2048]{1,0:T(8,128)(2,1)S(1)}, u32[]{:S(2)}, u32[]{:S(2)}) collective-permute-start(bf16[256,2048]{1,0:T(8,128)(2,1)S(1)} %get-tuple-element.48), channel_id=1, source_target_pairs={{0,1},{3,2},{4,5},{7,6},{8,9},{11,10},{12,13},{15,14},{16,17},{19,... | collective-permute-start | bytes 3145736 | tf_op jit(solution)/shard_map/ppermute | solution.py:346
  63.4 9.4 %collective-permute-done.17 = bf16[256,1536]{1,0:T(8,128)(2,1)S(1)} collective-permute-done((bf16[256,1536]{1,0:T(8,128)(2,1)S(1)}, bf16[256,1536]{1,0:T(8,128)(2,1)S(1)}, u32[]{:S(2)}, u32[]{:S(2)}) %collective-permute-start.17) | collective-permute-done | bytes 786464 | tf_op jit(solution)/shard_map/ppermute | solution.py:346
  72.8 0.0 collective-permute-done.18.o2
  72.8 0.0 collective-permute-done.19.e2
  72.8 1.3 %collective-permute-start.21 = (bf16[128,3584]{1,0:T(8,128)(2,1)S(1)}, bf16[128,3584]{1,0:T(8,128)(2,1)S(1)}, u32[]{:S(2)}, u32[]{:S(2)}) collective-permute-start(bf16[128,3584]{1,0:T(8,128)(2,1)S(1)} %collective-permute-done.18.o2), channel_id=1, source_target_pairs={{1,0},{2,3},{5,4},{6,7},{9,8},{10,11},{13,12},{14,15},{17,16},{18,... | collective-permute-start | bytes 2752520 | tf_op jit(solution)/shard_map/ppermute | solution.py:346
  74.1 0.2 add_convert_fusion
  74.3 0.7 collective-permute-start.20
  75.0 15.5 %collective-permute-done.15 = bf16[256,2048]{1,0:T(8,128)(2,1)S(1)} collective-permute-done((bf16[256,2048]{1,0:T(8,128)(2,1)S(1)}, bf16[256,2048]{1,0:T(8,128)(2,1)S(1)}, u32[]{:S(2)}, u32[]{:S(2)}) %collective-permute-start.15) | collective-permute-done | bytes 1048608 | tf_op jit(solution)/shard_map/ppermute | solution.py:346
  90.6 0.4 add_convert_fusion.4
  90.9 0.7 collective-permute-start.16
  91.7 0.0 collective-permute-done.21.e3
  91.7 0.1 add_convert_fusion.6
  91.8 4.5 %collective-permute-start.22 = (bf16[128,1536]{1,0:T(8,128)(2,1)S(1)}, bf16[128,1536]{1,0:T(8,128)(2,1)S(1)}, u32[]{:S(2)}, u32[]{:S(2)}) collective-permute-start(bf16[128,1536]{1,0:T(8,128)(2,1)S(1)} %add_convert_fusion.6), channel_id=1, source_target_pairs={{0,1},{1,0},{2,3},{3,2},{4,5},{5,4},{6,7},{7,6},{8,9},{9,8},{10,11... | collective-permute-start | bytes 1179656 | tf_op jit(solution)/shard_map/ppermute | solution.py:27
  96.3 0.6 transposed.1.q_t
  96.9 0.7 collective-permute-start.24
  97.6 6.7 %weight_gradient.2.refs_0_ = f32[2048,3584]{1,0:T(8,128)} custom-call(bf16[2048,512]{1,0:T(8,128)(2,1)S(1)} %transposed.1.q_t, bf16[128,3584]{1,0:T(8,128)(2,1)S(1)} %copy-done, bf16[128,3584]{1,0:T(8,128)(2,1)S(1)} %collective-permute-done.13.e1, bf16[128,3584]{1,0:T(8,128)(2,1)S(1)} %collective-permute-done.14.o1, ...), custom_call_target="tpu_custom_call" | custom-call | flops 3221225472 | bytes 16252928 | tf_op jit(solution)/shard_map/weight_gradient/pallas_call | solution.py:320
  104.3 0.0 collective-permute-done.22
  104.3 0.1 add_convert_fusion.3
  104.5 5.9 %collective-permute-start.23 = (bf16[128,2048]{1,0:T(8,128)(2,1)S(1)}, bf16[128,2048]{1,0:T(8,128)(2,1)S(1)}, u32[]{:S(2)}, u32[]{:S(2)}) collective-permute-start(bf16[128,2048]{1,0:T(8,128)(2,1)S(1)} %add_convert_fusion.3), channel_id=1, source_target_pairs={{0,1},{1,0},{2,3},{3,2},{4,5},{5,4},{6,7},{7,6},{8,9},{9,8},{10,11... | collective-permute-start | bytes 1572872 | tf_op jit(solution)/shard_map/ppermute | solution.py:27
  110.4 8.1 %weight_gradient.3 = f32[2048,3584]{1,0:T(8,128)} custom-call(bf16[2048,512]{1,0:T(8,128)(2,1)S(1)} %transposed.1.q_t, bf16[128,3584]{1,0:T(8,128)(2,1)S(1)} %copy-done, bf16[128,3584]{1,0:T(8,128)(2,1)S(1)} %collective-permute-done.13.e1, bf16[128,3584]{1,0:T(8,128)(2,1)S(1)} %collective-permute-done.14.o1, ...), custom_call_target="tpu_custom_call", output_to_operand_aliasing={{}: (7, {})} | custom-call | flops 4294967296 | bytes 20971520 | tf_op jit(solution)/shard_map/weight_gradient/pallas_call | solution.py:320
  118.5 0.1 add_convert_fusion.5
  118.6 0.0 collective-permute-done.24
  118.6 0.2 add_convert_fusion.1
  118.9 1.0 pad_maximum_fusion
  (10 shorter events, 0.1 us)
Async XLA Ops:
  0.6 24.7 %copy-start = (bf16[128,3584]{1,0:T(8,128)(2,1)S(1)}, bf16[128,3584]{1,0:T(8,128)(2,1)}, u32[]{:S(2)}) copy-start(bf16[128,3584]{1,0:T(8,128)(2,1)} %own_ref.3) | copy-start | bytes 2752516
  0.6 1.0 copy-start.1
  1.7 0.7 copy-start.2
  2.4 6.0 %collective-permute-start = (bf16[16,2048]{1,0:T(8,128)(2,1)S(1)}, bf16[16,2048]{1,0:T(8,128)(2,1)S(1)}, u32[]{:S(2)}, u32[]{:S(2)}) collective-permute-start(bf16[16,2048]{1,0:T(8,128)(2,1)S(1)} %get-tuple-element.35), channel_id=1, source_target_pairs={{0,1},{1,0},{2,3},{3,2},{4,5},{5,4},{6,7},{7,6},{8,9},{9,8},{10,11... | collective-permute-start | bytes 196616 | tf_op jit(solution)/shard_map/ppermute | solution.py:27
  5.5 7.3 %collective-permute-start.1 = (bf16[16,2048]{1,0:T(8,128)(2,1)S(1)}, bf16[16,2048]{1,0:T(8,128)(2,1)S(1)}, u32[]{:S(2)}, u32[]{:S(2)}) collective-permute-start(bf16[16,2048]{1,0:T(8,128)(2,1)S(1)} %get-tuple-element.36), channel_id=1, source_target_pairs={{0,2},{1,3},{2,0},{3,1},{4,6},{5,7},{6,4},{7,5},{8,10},{9,11},{10,... | collective-permute-start | bytes 196616 | tf_op jit(solution)/shard_map/ppermute | solution.py:27
  8.1 6.1 %collective-permute-start.2 = (bf16[16,2048]{1,0:T(8,128)(2,1)S(1)}, bf16[16,2048]{1,0:T(8,128)(2,1)S(1)}, u32[]{:S(2)}, u32[]{:S(2)}) collective-permute-start(bf16[16,2048]{1,0:T(8,128)(2,1)S(1)} %get-tuple-element.37), channel_id=1, source_target_pairs={{0,3},{1,2},{2,1},{3,0},{4,7},{5,6},{6,5},{7,4},{8,11},{9,10},{10,... | collective-permute-start | bytes 196616 | tf_op jit(solution)/shard_map/ppermute | solution.py:27
  14.5 6.0 %collective-permute-start.4 = (bf16[16,2048]{1,0:T(8,128)(2,1)S(1)}, bf16[16,2048]{1,0:T(8,128)(2,1)S(1)}, u32[]{:S(2)}, u32[]{:S(2)}) collective-permute-start(bf16[16,2048]{1,0:T(8,128)(2,1)S(1)} %get-tuple-element.40), channel_id=1, source_target_pairs={{0,2},{1,3},{2,0},{3,1},{4,6},{5,7},{6,4},{7,5},{8,10},{9,11},{10,... | collective-permute-start | bytes 196616 | tf_op jit(solution)/shard_map/ppermute | solution.py:27
  16.1 6.1 %collective-permute-start.5 = (bf16[16,2048]{1,0:T(8,128)(2,1)S(1)}, bf16[16,2048]{1,0:T(8,128)(2,1)S(1)}, u32[]{:S(2)}, u32[]{:S(2)}) collective-permute-start(bf16[16,2048]{1,0:T(8,128)(2,1)S(1)} %get-tuple-element.41), channel_id=1, source_target_pairs={{0,3},{1,2},{2,1},{3,0},{4,7},{5,6},{6,5},{7,4},{8,11},{9,10},{10,... | collective-permute-start | bytes 196616 | tf_op jit(solution)/shard_map/ppermute | solution.py:27
  16.8 5.4 %collective-permute-start.3 = (bf16[16,2048]{1,0:T(8,128)(2,1)S(1)}, bf16[16,2048]{1,0:T(8,128)(2,1)S(1)}, u32[]{:S(2)}, u32[]{:S(2)}) collective-permute-start(bf16[16,2048]{1,0:T(8,128)(2,1)S(1)} %get-tuple-element.39), channel_id=1, source_target_pairs={{0,1},{1,0},{2,3},{3,2},{4,5},{5,4},{6,7},{7,6},{8,9},{9,8},{10,11... | collective-permute-start | bytes 196616 | tf_op jit(solution)/shard_map/ppermute | solution.py:27
  22.3 6.4 %collective-permute-start.7 = (bf16[64,2048]{1,0:T(8,128)(2,1)S(1)}, bf16[64,2048]{1,0:T(8,128)(2,1)S(1)}, u32[]{:S(2)}, u32[]{:S(2)}) collective-permute-start(bf16[64,2048]{1,0:T(8,128)(2,1)S(1)} %pad_maximum_fusion.1.refs_0_), channel_id=1, source_target_pairs={{0,8},{4,12},{8,0},{12,4},{16,24},{20,28},{24,16},{28,20},{1,9},{5... | collective-permute-start | bytes 786440 | tf_op jit(solution)/shard_map/ppermute | solution.py:27
  23.8 6.4 %collective-permute-start.8 = (bf16[64,2048]{1,0:T(8,128)(2,1)S(1)}, bf16[64,2048]{1,0:T(8,128)(2,1)S(1)}, u32[]{:S(2)}, u32[]{:S(2)}) collective-permute-start(bf16[64,2048]{1,0:T(8,128)(2,1)S(1)} %pad_maximum_fusion.1.refs_0_), channel_id=1, source_target_pairs={{0,16},{4,20},{8,24},{12,28},{16,0},{20,4},{24,8},{28,12},{1,17},{... | collective-permute-start | bytes 786440 | tf_op jit(solution)/shard_map/ppermute | solution.py:27
  25.4 19.1 %collective-permute-start.13 = (bf16[128,3584]{1,0:T(8,128)(2,1)S(1)}, bf16[128,3584]{1,0:T(8,128)(2,1)S(1)}, u32[]{:S(2)}, u32[]{:S(2)}) collective-permute-start(bf16[128,3584]{1,0:T(8,128)(2,1)S(1)} %copy-done), channel_id=1, source_target_pairs={{0,1},{1,0},{2,3},{3,2},{4,5},{5,4},{6,7},{7,6},{8,9},{9,8},{10,11... | collective-permute-start | bytes 2752520 | tf_op jit(solution)/shard_map/ppermute | solution.py:27
  25.5 19.0 %collective-permute-start.14 = (bf16[128,3584]{1,0:T(8,128)(2,1)S(1)}, bf16[128,3584]{1,0:T(8,128)(2,1)S(1)}, u32[]{:S(2)}, u32[]{:S(2)}) collective-permute-start(bf16[128,3584]{1,0:T(8,128)(2,1)S(1)} %copy-done), channel_id=1, source_target_pairs={{1,2},{2,1},{5,6},{6,5},{9,10},{10,9},{13,14},{14,13},{17,18},{18,... | collective-permute-start | bytes 2752520 | tf_op jit(solution)/shard_map/ppermute | solution.py:346
  26.2 5.7 %collective-permute-start.6 = (bf16[64,2048]{1,0:T(8,128)(2,1)S(1)}, bf16[64,2048]{1,0:T(8,128)(2,1)S(1)}, u32[]{:S(2)}, u32[]{:S(2)}) collective-permute-start(bf16[64,2048]{1,0:T(8,128)(2,1)S(1)} %pad_maximum_fusion.1.refs_0_), channel_id=1, source_target_pairs={{0,4},{4,0},{8,12},{12,8},{16,20},{20,16},{24,28},{28,24},{1,5},{5... | collective-permute-start | bytes 786440 | tf_op jit(solution)/shard_map/ppermute | solution.py:27
  30.2 6.4 %collective-permute-start.11 = (bf16[64,2048]{1,0:T(8,128)(2,1)S(1)}, bf16[64,2048]{1,0:T(8,128)(2,1)S(1)}, u32[]{:S(2)}, u32[]{:S(2)}) collective-permute-start(bf16[64,2048]{1,0:T(8,128)(2,1)S(1)} %broadcast_select_fusion), channel_id=1, source_target_pairs={{0,16},{4,12},{8,24},{12,4},{16,0},{20,28},{24,8},{28,20},{1,17},{... | collective-permute-start | bytes 786440 | tf_op jit(solution)/shard_map/ppermute | solution.py:162
  31.8 4.9 %collective-permute-start.9 = (bf16[64,2048]{1,0:T(8,128)(2,1)S(1)}, bf16[64,2048]{1,0:T(8,128)(2,1)S(1)}, u32[]{:S(2)}, u32[]{:S(2)}) collective-permute-start(bf16[64,2048]{1,0:T(8,128)(2,1)S(1)} %collective-permute-done.7.refs_2_), channel_id=1, source_target_pairs={{0,4},{4,0},{8,12},{12,8},{16,20},{20,16},{24,28},{28,24},{1,5},{5... | collective-permute-start | bytes 786440 | tf_op jit(solution)/shard_map/ppermute | solution.py:27
  31.8 4.9 %collective-permute-start.10 = (bf16[64,2048]{1,0:T(8,128)(2,1)S(1)}, bf16[64,2048]{1,0:T(8,128)(2,1)S(1)}, u32[]{:S(2)}, u32[]{:S(2)}) collective-permute-start(bf16[64,2048]{1,0:T(8,128)(2,1)S(1)} %collective-permute-done.8.refs_4_), channel_id=1, source_target_pairs={{0,4},{4,0},{8,12},{12,8},{16,20},{20,16},{24,28},{28,24},{1,5},{5... | collective-permute-start | bytes 786440 | tf_op jit(solution)/shard_map/ppermute | solution.py:27
  36.7 1.5 %collective-permute-start.12 = (bf16[64,2048]{1,0:T(8,128)(2,1)S(1)}, bf16[64,2048]{1,0:T(8,128)(2,1)S(1)}, u32[]{:S(2)}, u32[]{:S(2)}) collective-permute-start(bf16[64,2048]{1,0:T(8,128)(2,1)S(1)} %collective-permute-done.11.refs_6_), channel_id=1, source_target_pairs={{0,4},{4,0},{8,12},{12,8},{16,20},{20,16},{24,28},{28,24},{1,5},{5... | collective-permute-start | bytes 786440 | tf_op jit(solution)/shard_map/ppermute | solution.py:27
  44.5 28.3 %collective-permute-start.18 = (bf16[128,3584]{1,0:T(8,128)(2,1)S(1)}, bf16[128,3584]{1,0:T(8,128)(2,1)S(1)}, u32[]{:S(2)}, u32[]{:S(2)}) collective-permute-start(bf16[128,3584]{1,0:T(8,128)(2,1)S(1)} %collective-permute-done.13.e1), channel_id=1, source_target_pairs={{1,2},{2,1},{5,6},{6,5},{9,10},{10,9},{13,14},{14,13},{17,18},{18,... | collective-permute-start | bytes 2752520 | tf_op jit(solution)/shard_map/ppermute | solution.py:346
  45.2 27.6 %collective-permute-start.19 = (bf16[128,3584]{1,0:T(8,128)(2,1)S(1)}, bf16[128,3584]{1,0:T(8,128)(2,1)S(1)}, u32[]{:S(2)}, u32[]{:S(2)}) collective-permute-start(bf16[128,3584]{1,0:T(8,128)(2,1)S(1)} %collective-permute-done.14.o1), channel_id=1, source_target_pairs={{1,0},{2,3},{5,4},{6,7},{9,8},{10,11},{13,12},{14,15},{17,16},{18,... | collective-permute-start | bytes 2752520 | tf_op jit(solution)/shard_map/ppermute | solution.py:346
  46.5 26.3 %collective-permute-start.17 = (bf16[256,1536]{1,0:T(8,128)(2,1)S(1)}, bf16[256,1536]{1,0:T(8,128)(2,1)S(1)}, u32[]{:S(2)}, u32[]{:S(2)}) collective-permute-start(bf16[256,1536]{1,0:T(8,128)(2,1)S(1)} %get-tuple-element.49), channel_id=1, source_target_pairs={{0,1},{3,2},{4,5},{7,6},{8,9},{11,10},{12,13},{15,14},{16,17},{19,... | collective-permute-start | bytes 2359304 | tf_op jit(solution)/shard_map/ppermute | solution.py:346
  62.0 28.5 %collective-permute-start.15 = (bf16[256,2048]{1,0:T(8,128)(2,1)S(1)}, bf16[256,2048]{1,0:T(8,128)(2,1)S(1)}, u32[]{:S(2)}, u32[]{:S(2)}) collective-permute-start(bf16[256,2048]{1,0:T(8,128)(2,1)S(1)} %get-tuple-element.48), channel_id=1, source_target_pairs={{0,1},{3,2},{4,5},{7,6},{8,9},{11,10},{12,13},{15,14},{16,17},{19,... | collective-permute-start | bytes 3145736 | tf_op jit(solution)/shard_map/ppermute | solution.py:346
  72.8 18.8 %collective-permute-start.21 = (bf16[128,3584]{1,0:T(8,128)(2,1)S(1)}, bf16[128,3584]{1,0:T(8,128)(2,1)S(1)}, u32[]{:S(2)}, u32[]{:S(2)}) collective-permute-start(bf16[128,3584]{1,0:T(8,128)(2,1)S(1)} %collective-permute-done.18.o2), channel_id=1, source_target_pairs={{1,0},{2,3},{5,4},{6,7},{9,8},{10,11},{13,12},{14,15},{17,16},{18,... | collective-permute-start | bytes 2752520 | tf_op jit(solution)/shard_map/ppermute | solution.py:346
  74.3 17.4 %collective-permute-start.20 = (bf16[256,1536]{1,0:T(8,128)(2,1)S(1)}, bf16[256,1536]{1,0:T(8,128)(2,1)S(1)}, u32[]{:S(2)}, u32[]{:S(2)}) collective-permute-start(bf16[256,1536]{1,0:T(8,128)(2,1)S(1)} %add_convert_fusion), channel_id=1, source_target_pairs={{1,2},{2,1},{5,6},{6,5},{9,10},{10,9},{13,14},{14,13},{17,18},{18,... | collective-permute-start | bytes 2359304 | tf_op jit(solution)/shard_map/ppermute | solution.py:346
  90.9 13.4 %collective-permute-start.16 = (bf16[128,2048]{1,0:T(8,128)(2,1)S(1)}, bf16[128,2048]{1,0:T(8,128)(2,1)S(1)}, u32[]{:S(2)}, u32[]{:S(2)}) collective-permute-start(bf16[128,2048]{1,0:T(8,128)(2,1)S(1)} %get-tuple-element.66), channel_id=1, source_target_pairs={{1,2},{2,1},{5,6},{6,5},{9,10},{10,9},{13,14},{14,13},{17,18},{18,... | collective-permute-start | bytes 1572872 | tf_op jit(solution)/shard_map/ppermute | solution.py:346
  91.8 12.6 %collective-permute-start.22 = (bf16[128,1536]{1,0:T(8,128)(2,1)S(1)}, bf16[128,1536]{1,0:T(8,128)(2,1)S(1)}, u32[]{:S(2)}, u32[]{:S(2)}) collective-permute-start(bf16[128,1536]{1,0:T(8,128)(2,1)S(1)} %add_convert_fusion.6), channel_id=1, source_target_pairs={{0,1},{1,0},{2,3},{3,2},{4,5},{5,4},{6,7},{7,6},{8,9},{9,8},{10,11... | collective-permute-start | bytes 1179656 | tf_op jit(solution)/shard_map/ppermute | solution.py:27
  96.9 21.7 %collective-permute-start.24 = (bf16[128,2048]{1,0:T(8,128)(2,1)S(1)}, bf16[128,2048]{1,0:T(8,128)(2,1)S(1)}, u32[]{:S(2)}, u32[]{:S(2)}) collective-permute-start(bf16[128,2048]{1,0:T(8,128)(2,1)S(1)} %get-tuple-element.67), channel_id=1, source_target_pairs={{1,2},{2,1},{5,6},{6,5},{9,10},{10,9},{13,14},{14,13},{17,18},{18,... | collective-permute-start | bytes 1572872 | tf_op jit(solution)/shard_map/ppermute | solution.py:346
  104.5 14.1 %collective-permute-start.23 = (bf16[128,2048]{1,0:T(8,128)(2,1)S(1)}, bf16[128,2048]{1,0:T(8,128)(2,1)S(1)}, u32[]{:S(2)}, u32[]{:S(2)}) collective-permute-start(bf16[128,2048]{1,0:T(8,128)(2,1)S(1)} %add_convert_fusion.3), channel_id=1, source_target_pairs={{0,1},{1,0},{2,3},{3,2},{4,5},{5,4},{6,7},{7,6},{8,9},{9,8},{10,11... | collective-permute-start | bytes 1572872 | tf_op jit(solution)/shard_map/ppermute | solution.py:27

commit v3 on v2

--- a/solution.py
+++ b/solution.py
@@ -63,10 +63,6 @@
     return (projected, weight_grad)
 
 
-def parity_sign(bits):
-    return (1 - 2 * ((bits ^ bits >> 1) & 1)).astype(jnp.float32)
-
-
 def butterfly(parts):
     stride = 1
     parts = list(parts)
@@ -92,67 +88,54 @@
     return list(lax.optimization_barrier(tuple(arrays) + tuple(earlier))[: len(arrays)])
 
 
-def sign_kernel(x_ref, bits_ref, *outs):
-    z = lax.axis_index("tensor")
-    rows = outs[0].shape[0]
+def sign_kernel(x_ref, bits_ref, out_ref):
     sign = (1 - 2 * bits_ref[...]).astype(jnp.float32)
-    for m, out in enumerate(outs):
-        first = pl.multiple_of((z ^ m) * rows, rows)
-        out[...] = (x_ref[pl.ds(first, rows), :].astype(jnp.float32) * sign).astype(out.dtype)
+    rows = out_ref.shape[1]
+    for group in range(out_ref.shape[0]):
+        piece = x_ref[group * rows : (group + 1) * rows, :].astype(jnp.float32) * sign
+        out_ref[group] = piece.astype(out_ref.dtype)
 
 
 def signed_pieces(x, sign_bits, groups):
     rows, width = x.shape
-    part = rows // groups
     return pl.pallas_call(
         sign_kernel,
-        out_shape=[jax.ShapeDtypeStruct((part, width), jnp.bfloat16)] * groups,
+        out_shape=jax.ShapeDtypeStruct((groups, rows // groups, width), jnp.bfloat16),
         in_specs=[VMEM] * 2,
-        out_specs=[VMEM] * groups,
+        out_specs=VMEM,
         compiler_params=pltpu.CompilerParams(vmem_limit_bytes=8 * MIB),
         name="signed_pieces",
     )(x, sign_bits.reshape(1, width))
 
 
-def rotate_kernel(groups, order, factor, h_ref, *refs):
-    pieces, outs = refs[:groups], refs[groups:]
-    z = lax.axis_index("tensor")
-    rows, width = pieces[0].shape
+def rotate_kernel(order, factor, h_ref, x_ref, out_ref):
+    groups, rows, width = x_ref.shape
     chunks = width // order
     stacked = jnp.concatenate(
-        [piece[:, j * order : (j + 1) * order] for piece in pieces for j in range(chunks)], axis=0
+        [x_ref[i, :, j * order : (j + 1) * order] for i in range(groups) for j in range(chunks)],
+        axis=0,
     )
     product = jnp.dot(stacked, h_ref[...], preferred_element_type=jnp.float32)
-    rotated = []
-    for i in range(groups):
-        sign = parity_sign(z & i)
-        rotated.append(
-            butterfly(
-                [
-                    product[(i * chunks + j) * rows : (i * chunks + j + 1) * rows] * sign
-                    for j in range(chunks)
-                ]
-            )
-        )
+    rotated = [
+        butterfly([product[n * rows : (n + 1) * rows] for n in range(i * chunks, (i + 1) * chunks)])
+        for i in range(groups)
+    ]
     for j in range(chunks):
-        panel = butterfly([r[j] for r in rotated])
-        for m in range(groups):
-            scale = parity_sign((z ^ m) & z) * factor
-            outs[m][:, j * order : (j + 1) * order] = (panel[m] * scale).astype(jnp.bfloat16)
-
-
-def rotate(pieces):
-    groups = len(pieces)
-    rows, width = pieces[0].shape
+        for i, panel in enumerate(butterfly([r[j] for r in rotated])):
+            out_ref[i, :, j * order : (j + 1) * order] = (panel * factor).astype(out_ref.dtype)
+
+
+def rotate(panels):
+    groups, rows, width = panels.shape
     order = min(256, width)
     return pl.pallas_call(
-        functools.partial(rotate_kernel, groups, order, 1.0 / math.sqrt(width * groups)),
-        out_shape=[jax.ShapeDtypeStruct((rows, width), jnp.bfloat16)] * groups,
-        in_specs=[VMEM] * (1 + groups),
-        out_specs=[VMEM] * groups,
+        functools.partial(rotate_kernel, order, 1.0 / math.sqrt(width * groups)),
+        out_shape=jax.ShapeDtypeStruct(panels.shape, jnp.bfloat16),
+        in_specs=[VMEM] * 2,
+        out_specs=VMEM,
         compiler_params=pltpu.CompilerParams(vmem_limit_bytes=8 * MIB),
         name="rotate",
-    )(hadamard(order), *pieces)
+    )(hadamard(order), panels)
 
 
 def gather_rows(own, d):
@@ -358,16 +341,10 @@
     rows = x_tokens.shape[0]
     hidden = weight.shape[1]
 
-    pieces = list(signed_pieces(x_tokens, sign_bits, groups))
-    for m in (3, 2, 1):
-        pieces[m] = swap(pieces[m], "tensor", m)
-    turned = list(rotate(pieces))
-    (up,) = after([upstream], turned[0])
-    for m in (3, 2, 1):
-        turned[m] = swap(turned[m], "tensor", m)
-    own = jnp.concatenate(
-        [lax.select_n(z, *[turned[g ^ k] for k in range(groups)]) for g in range(groups)]
-    )
+    panels = signed_pieces(x_tokens, sign_bits, groups)
+    turned = rotate(lax.all_to_all(panels, "tensor", 0, 0))
+    (up,) = after([upstream], turned)
+    own = lax.all_to_all(turned, "tensor", 0, 0).reshape(x_tokens.shape)
 
     e1 = swap(up, "tensor", 1)
     o1 = move(up, *MIDDLE)
@@ -383,7 +360,7 @@
     own_b, pair_b, beyond_b = project(q, weight, cut, hidden - cut, (block, block, 2 * block))
 
     inward_a = move(beyond_a, *INWARD)
-    inward_b = move(beyond_b, *INWARD)
+    inward_b = move(after([beyond_b], inward_a)[0], *INWARD)
     inward_a, o2, e2 = after([inward_a, o2, e2])
     across_a = move(total(beyond_a, inward_a), *MIDDLE)
     e3 = move(o2, *OUTWARD)

time: 120 us -> 127 us (1.058)
  blocking collectives: 0 us -> 10.6 us
  starting transfers between devices: 40.8 us -> 33.5 us
  waiting for transfers between devices: 44.9 us -> 47.1 us
    all_to_all x0 -> x1, blocking collectives: none -> 10.6 us  [lined(): own = lax.all_to_all(turned, 'tensor', 0, 0).reshape(x_tokens.shape)]
    ppermute x15 -> x9, starting transfers between devices: 23.4 us -> 12.9 us  [swap(): lax.ppermute(block, axis, [(i, i ^ mask) for i in range(count) if i ^ mas...]
    ppermute x15 -> x9, waiting for transfers between devices: 15.6 us -> 5.38 us  [swap(): lax.ppermute(block, axis, [(i, i ^ mask) for i in range(count) if i ^ mas...]
    all_to_all x0 -> x1, waiting for transfers between devices: none -> 8.58 us  [lined(): turned = rotate(lax.all_to_all(panels, 'tensor', 0, 0))]
    all_to_all x0 -> x1, starting transfers between devices: none -> 6.32 us  [lined(): turned = rotate(lax.all_to_all(panels, 'tensor', 0, 0))]
    ppermute x9, waiting for transfers between devices: 25 us -> 28.8 us  [move(): return lax.ppermute(block, 'tensor', pairs)]
    ppermute x9, starting transfers between devices: 15.8 us -> 12.7 us  [move(): return lax.ppermute(block, 'tensor', pairs)]
  transfers between devices with their start and end apart: 25 -> 20, of which waited for: 11 -> 9; matrix products, arithmetic and copies ran while one was open for 1% -> 1% of each run, Pallas kernels for 24% -> 23%
where the time goes in v3:
time: 127 us; the launch traced here: 126 us
  waiting for transfers between devices  47.1 us (37%)
  starting transfers between devices  33.5 us (26%)
  Pallas kernels  29.7 us (23%)
  blocking collectives  10.6 us (8%)
  other arithmetic  2.53 us (2%)
  local copies, waits for them, and re-layouts  1.72 us (1%)
    ppermute x9, waiting for transfers between devices, move(): return lax.ppermute(block, 'tensor', pairs)  28.8 us
    pallas_call x2, Pallas kernels, weight_gradient(): pl.pallas_call(functools.partial(grad_kernel, tile, start), out_shape=jax...  14.8 us
    ppermute x9, starting transfers between devices, swap(): lax.ppermute(block, axis, [(i, i ^ mask) for i in range(count) if i ^ mas...  12.9 us
    ppermute x9, starting transfers between devices, move(): return lax.ppermute(block, 'tensor', pairs)  12.7 us
    all_to_all x1, blocking collectives, lined(): own = lax.all_to_all(turned, 'tensor', 0, 0).reshape(x_tokens.shape)  10.6 us
    all_to_all x1, waiting for transfers between devices, lined(): turned = rotate(lax.all_to_all(panels, 'tensor', 0, 0))  8.58 us
    pallas_call x1, Pallas kernels, project(): pl.pallas_call(project_kernel, out_shape=[jax.ShapeDtypeStruct((block, wi...  7.14 us
    all_to_all x1, starting transfers between devices, lined(): turned = rotate(lax.all_to_all(panels, 'tensor', 0, 0))  6.32 us
  transfers between devices with their start and end apart: 20, of which 9 were waited for; matrix products, arithmetic and copies ran while one was open for 1% of the time, Pallas kernels for 23%

profile of v3, /device:TPU:0, one launch (start us, length us, event | category | flops | bytes accessed | tf_op | source)
XLA Modules:
  0.0 126.0 jit_solution(1807112579036620564)
XLA Ops:
  0.6 0.0 copy-start
  0.6 0.0 copy-start.1
  0.6 1.0 copy-done.1
  1.7 0.0 copy-start.2
  1.7 0.7 copy-done.2
  2.4 0.7 signed_pieces.1
  3.1 6.3 %all-to-all-start = ((bf16[4,16,2048]{2,1,0:T(8,128)(2,1)}), bf16[4,16,2048]{2,1,0:T(8,128)(2,1)S(1)}, u32[]{:S(2)}, u32[]{:S(2)}) async-start(bf16[4,16,2048]{2,1,0:T(8,128)(2,1)} %signed_pieces.1), calls=%async_computation | async-start | bytes 524288 | tf_op jit(solution)/shard_map/all_to_all | solution.py:345
  9.4 0.3 fusion.3.h_ref
  9.8 8.6 %all-to-all-done.x_ref = bf16[4,16,2048]{2,1,0:T(8,128)(2,1)S(1)} async-done(((bf16[4,16,2048]{2,1,0:T(8,128)(2,1)}), bf16[4,16,2048]{2,1,0:T(8,128)(2,1)S(1)}, u32[]{:S(2)}, u32[]{:S(2)}) %all-to-all-start) | async-done | bytes 262176 | tf_op jit(solution)/shard_map/all_to_all | solution.py:345
  18.4 0.3 rotate.1
  18.7 10.6 %all_to_all.10 = bf16[4,16,2048]{2,1,0:T(8,128)(2,1)S(1)} all-to-all(bf16[4,16,2048]{2,1,0:T(8,128)(2,1)S(1)} %rotate.1), channel_id=1, replica_groups=mesh['dp'=8,'tensor'=4] {'tensor'}, dimensions={0} | all-to-all | bytes 524288 | tf_op jit(solution)/shard_map/all_to_all | solution.py:347
  29.3 1.5 %collective-permute-start.1 = (bf16[64,2048]{1,0:T(8,128)(2,1)S(1)}, bf16[64,2048]{1,0:T(8,128)(2,1)S(1)}, u32[]{:S(2)}, u32[]{:S(2)}) collective-permute-start(bf16[64,2048]{1,0:T(8,128)(2,1)S(1)} %bitcast.2), channel_id=1, source_target_pairs={{0,8},{4,12},{8,0},{12,4},{16,24},{20,28},{24,16},{28,20},{1,9},{5... | collective-permute-start | bytes 786440 | tf_op jit(solution)/shard_map/ppermute | solution.py:27
  30.7 1.5 %collective-permute-start.2 = (bf16[64,2048]{1,0:T(8,128)(2,1)S(1)}, bf16[64,2048]{1,0:T(8,128)(2,1)S(1)}, u32[]{:S(2)}, u32[]{:S(2)}) collective-permute-start(bf16[64,2048]{1,0:T(8,128)(2,1)S(1)} %bitcast.3), channel_id=1, source_target_pairs={{0,16},{4,20},{8,24},{12,28},{16,0},{20,4},{24,8},{28,12},{1,17},{... | collective-permute-start | bytes 786440 | tf_op jit(solution)/shard_map/ppermute | solution.py:27
  32.3 0.0 copy-done
  32.3 0.2 collective-permute-start.7
  32.5 0.7 collective-permute-start.8
  33.2 0.1 collective-permute-start
  33.3 2.4 %collective-permute-done.1.refs_2_ = bf16[64,2048]{1,0:T(8,128)(2,1)S(1)} collective-permute-done((bf16[64,2048]{1,0:T(8,128)(2,1)S(1)}, bf16[64,2048]{1,0:T(8,128)(2,1)S(1)}, u32[]{:S(2)}, u32[]{:S(2)}) %collective-permute-start.1) | collective-permute-done | bytes 262176 | tf_op jit(solution)/shard_map/ppermute | solution.py:27
  35.6 1.5 %collective-permute-done.2.refs_4_ = bf16[64,2048]{1,0:T(8,128)(2,1)S(1)} collective-permute-done((bf16[64,2048]{1,0:T(8,128)(2,1)S(1)}, bf16[64,2048]{1,0:T(8,128)(2,1)S(1)}, u32[]{:S(2)}, u32[]{:S(2)}) %collective-permute-start.2) | collective-permute-done | bytes 262176 | tf_op jit(solution)/shard_map/ppermute | solution.py:27
  37.1 1.6 %collective-permute-start.5 = (bf16[64,2048]{1,0:T(8,128)(2,1)S(1)}, bf16[64,2048]{1,0:T(8,128)(2,1)S(1)}, u32[]{:S(2)}, u32[]{:S(2)}) collective-permute-start(bf16[64,2048]{1,0:T(8,128)(2,1)S(1)} %broadcast_select_fusion), channel_id=1, source_target_pairs={{0,16},{4,12},{8,24},{12,4},{16,0},{20,28},{24,8},{28,20},{1,17},{... | collective-permute-start | bytes 786440 | tf_op jit(solution)/shard_map/ppermute | solution.py:145
  38.7 0.0 collective-permute-start.3
  38.8 0.0 collective-permute-done.refs_1_
  38.8 0.5 collective-permute-start.4
  39.3 4.3 %collective-permute-done.5.refs_6_ = bf16[64,2048]{1,0:T(8,128)(2,1)S(1)} collective-permute-done((bf16[64,2048]{1,0:T(8,128)(2,1)S(1)}, bf16[64,2048]{1,0:T(8,128)(2,1)S(1)}, u32[]{:S(2)}, u32[]{:S(2)}) %collective-permute-start.5) | collective-permute-done | bytes 262176 | tf_op jit(solution)/shard_map/ppermute | solution.py:145
  43.6 0.0 collective-permute-start.6
  43.6 0.0 collective-permute-done.3.refs_3_
  43.6 0.0 collective-permute-done.4.refs_5_
  43.6 1.5 %collective-permute-done.6.refs_7_ = bf16[64,2048]{1,0:T(8,128)(2,1)S(1)} collective-permute-done((bf16[64,2048]{1,0:T(8,128)(2,1)S(1)}, bf16[64,2048]{1,0:T(8,128)(2,1)S(1)}, u32[]{:S(2)}, u32[]{:S(2)}) %collective-permute-start.6) | collective-permute-done | bytes 262176 | tf_op jit(solution)/shard_map/ppermute | solution.py:27
  45.1 6.0 %project_first.1 = (bf16[512,2048]{1,0:T(8,128)(2,1)S(1)}, bf16[128,1536]{1,0:T(8,128)(2,1)S(1)}, bf16[128,1536]{1,0:T(8,128)(2,1)S(1)}, bf16[256,1536]{1,0:T(8,128)(2,1)S(1)}) custom-call(bf16[64,2048]{1,0:T(8,128)(2,1)S(1)} %bitcast.5, bf16[64,2048]{1,0:T(8,128)(2,1)S(1)} %collective-permute-done.refs_1_, ...), custom_call_target="tpu_custom_call" | custom-call | flops 1 | bytes 1 | tf_op jit(solution)/shard_map/project_first/pallas_call | solution.py:204
  51.2 2.2 %collective-permute-start.9 = (bf16[256,1536]{1,0:T(8,128)(2,1)S(1)}, bf16[256,1536]{1,0:T(8,128)(2,1)S(1)}, u32[]{:S(2)}, u32[]{:S(2)}) collective-permute-start(bf16[256,1536]{1,0:T(8,128)(2,1)S(1)} %get-tuple-element.34), channel_id=1, source_target_pairs={{0,1},{3,2},{4,5},{7,6},{8,9},{11,10},{12,13},{15,14},{16,17},{19,... | collective-permute-start | bytes 2359304 | tf_op jit(solution)/shard_map/ppermute | solution.py:329
  53.3 0.0 collective-permute-done.7.e1
  53.3 0.0 collective-permute-done.8.o1
  53.4 0.7 collective-permute-start.12
  54.1 1.3 %collective-permute-start.13 = (bf16[128,3584]{1,0:T(8,128)(2,1)S(1)}, bf16[128,3584]{1,0:T(8,128)(2,1)S(1)}, u32[]{:S(2)}, u32[]{:S(2)}) collective-permute-start(bf16[128,3584]{1,0:T(8,128)(2,1)S(1)} %collective-permute-done.8.o1), channel_id=1, source_target_pairs={{1,0},{2,3},{5,4},{6,7},{9,8},{10,11},{13,12},{14,15},{17,16},{18,... | collective-permute-start | bytes 2752520 | tf_op jit(solution)/shard_map/ppermute | solution.py:329
  55.4 7.1 %project.1 = (bf16[128,2048]{1,0:T(8,128)(2,1)S(1)}, bf16[128,2048]{1,0:T(8,128)(2,1)S(1)}, bf16[256,2048]{1,0:T(8,128)(2,1)S(1)}) custom-call(bf16[512,2048]{1,0:T(8,128)(2,1)S(1)} %get-tuple-element.39.q_ref, bf16[2048,3584]{1,0:T(8,128)(2,1)} %w_ref.1), custom_call_target="tpu_custom_call" | custom-call | flops 4294967296 | bytes 12582912 | tf_op jit(solution)/shard_map/project/pallas_call | solution.py:226
  62.5 7.8 %collective-permute-done.9 = bf16[256,1536]{1,0:T(8,128)(2,1)S(1)} collective-permute-done((bf16[256,1536]{1,0:T(8,128)(2,1)S(1)}, bf16[256,1536]{1,0:T(8,128)(2,1)S(1)}, u32[]{:S(2)}, u32[]{:S(2)}) %collective-permute-start.9) | collective-permute-done | bytes 786464 | tf_op jit(solution)/shard_map/ppermute | solution.py:329
  70.4 4.4 %collective-permute-start.10 = (bf16[256,2048]{1,0:T(8,128)(2,1)S(1)}, bf16[256,2048]{1,0:T(8,128)(2,1)S(1)}, u32[]{:S(2)}, u32[]{:S(2)}) collective-permute-start(bf16[256,2048]{1,0:T(8,128)(2,1)S(1)} %get-tuple-element.35), channel_id=1, source_target_pairs={{0,1},{3,2},{4,5},{7,6},{8,9},{11,10},{12,13},{15,14},{16,17},{19,... | collective-permute-start | bytes 3145736 | tf_op jit(solution)/shard_map/ppermute | solution.py:329
  74.8 0.0 collective-permute-done.12.o2
  74.8 3.5 %collective-permute-done.13.e2 = bf16[128,3584]{1,0:T(8,128)(2,1)S(1)} collective-permute-done((bf16[128,3584]{1,0:T(8,128)(2,1)S(1)}, bf16[128,3584]{1,0:T(8,128)(2,1)S(1)}, u32[]{:S(2)}, u32[]{:S(2)}) %collective-permute-start.13) | collective-permute-done | bytes 917536 | tf_op jit(solution)/shard_map/ppermute | solution.py:329
  78.4 1.3 %collective-permute-start.15 = (bf16[128,3584]{1,0:T(8,128)(2,1)S(1)}, bf16[128,3584]{1,0:T(8,128)(2,1)S(1)}, u32[]{:S(2)}, u32[]{:S(2)}) collective-permute-start(bf16[128,3584]{1,0:T(8,128)(2,1)S(1)} %collective-permute-done.12.o2), channel_id=1, source_target_pairs={{1,0},{2,3},{5,4},{6,7},{9,8},{10,11},{13,12},{14,15},{17,16},{18,... | collective-permute-start | bytes 2752520 | tf_op jit(solution)/shard_map/ppermute | solution.py:329
  79.6 0.2 add_convert_fusion
  79.8 0.7 collective-permute-start.14
  80.6 16.1 %collective-permute-done.10 = bf16[256,2048]{1,0:T(8,128)(2,1)S(1)} collective-permute-done((bf16[256,2048]{1,0:T(8,128)(2,1)S(1)}, bf16[256,2048]{1,0:T(8,128)(2,1)S(1)}, u32[]{:S(2)}, u32[]{:S(2)}) %collective-permute-start.10) | collective-permute-done | bytes 1048608 | tf_op jit(solution)/shard_map/ppermute | solution.py:329
  96.6 0.4 add_convert_fusion.4
  97.0 0.7 collective-permute-start.11
  97.7 0.0 collective-permute-done.14
  97.7 1.4 %collective-permute-done.15.e3 = bf16[128,3584]{1,0:T(8,128)(2,1)S(1)} collective-permute-done((bf16[128,3584]{1,0:T(8,128)(2,1)S(1)}, bf16[128,3584]{1,0:T(8,128)(2,1)S(1)}, u32[]{:S(2)}, u32[]{:S(2)}) %collective-permute-start.15) | collective-permute-done | bytes 917536 | tf_op jit(solution)/shard_map/ppermute | solution.py:329
  99.1 0.1 add_convert_fusion.6
  99.2 3.5 %collective-permute-start.16 = (bf16[128,1536]{1,0:T(8,128)(2,1)S(1)}, bf16[128,1536]{1,0:T(8,128)(2,1)S(1)}, u32[]{:S(2)}, u32[]{:S(2)}) collective-permute-start(bf16[128,1536]{1,0:T(8,128)(2,1)S(1)} %add_convert_fusion.6), channel_id=1, source_target_pairs={{0,1},{1,0},{2,3},{3,2},{4,5},{5,4},{6,7},{7,6},{8,9},{9,8},{10,11... | collective-permute-start | bytes 1179656 | tf_op jit(solution)/shard_map/ppermute | solution.py:27
  102.6 0.6 transposed.1.q_t
  103.2 0.7 collective-permute-start.18
  103.9 6.7 %weight_gradient.2.refs_0_ = f32[2048,3584]{1,0:T(8,128)} custom-call(bf16[2048,512]{1,0:T(8,128)(2,1)S(1)} %transposed.1.q_t, bf16[128,3584]{1,0:T(8,128)(2,1)S(1)} %copy-done, bf16[128,3584]{1,0:T(8,128)(2,1)S(1)} %collective-permute-done.7.e1, bf16[128,3584]{1,0:T(8,128)(2,1)S(1)} %collective-permute-done.8.o1, ...), custom_call_target="tpu_custom_call" | custom-call | flops 3221225472 | bytes 16252928 | tf_op jit(solution)/shard_map/weight_gradient/pallas_call | solution.py:303
  110.7 0.0 collective-permute-done.16
  110.7 0.0 collective-permute-done.11
  110.7 0.1 add_convert_fusion.3
  110.8 5.6 %collective-permute-start.17 = (bf16[128,2048]{1,0:T(8,128)(2,1)S(1)}, bf16[128,2048]{1,0:T(8,128)(2,1)S(1)}, u32[]{:S(2)}, u32[]{:S(2)}) collective-permute-start(bf16[128,2048]{1,0:T(8,128)(2,1)S(1)} %add_convert_fusion.3), channel_id=1, source_target_pairs={{0,1},{1,0},{2,3},{3,2},{4,5},{5,4},{6,7},{7,6},{8,9},{9,8},{10,11... | collective-permute-start | bytes 1572872 | tf_op jit(solution)/shard_map/ppermute | solution.py:27
  116.4 8.1 %weight_gradient.3 = f32[2048,3584]{1,0:T(8,128)} custom-call(bf16[2048,512]{1,0:T(8,128)(2,1)S(1)} %transposed.1.q_t, bf16[128,3584]{1,0:T(8,128)(2,1)S(1)} %copy-done, bf16[128,3584]{1,0:T(8,128)(2,1)S(1)} %collective-permute-done.7.e1, bf16[128,3584]{1,0:T(8,128)(2,1)S(1)} %collective-permute-done.8.o1, ...), custom_call_target="tpu_custom_call", output_to_operand_aliasing={{}: (7, {})} | custom-call | flops 4294967296 | bytes 20971520 | tf_op jit(solution)/shard_map/weight_gradient/pallas_call | solution.py:303
  124.6 0.1 add_convert_fusion.5
  124.7 0.0 collective-permute-done.18
  124.7 0.0 collective-permute-done.17
  124.7 0.2 add_convert_fusion.1
  125.0 1.0 pad_maximum_fusion
  (1 shorter events, 0.0 us)
Async XLA Ops:
  0.6 31.6 %copy-start = (bf16[128,3584]{1,0:T(8,128)(2,1)S(1)}, bf16[128,3584]{1,0:T(8,128)(2,1)}, u32[]{:S(2)}) copy-start(bf16[128,3584]{1,0:T(8,128)(2,1)} %own_ref.3) | copy-start | bytes 2752516
  0.6 1.0 copy-start.1
  1.7 0.7 copy-start.2
  3.1 15.2 %all-to-all-start = ((bf16[4,16,2048]{2,1,0:T(8,128)(2,1)}), bf16[4,16,2048]{2,1,0:T(8,128)(2,1)S(1)}, u32[]{:S(2)}, u32[]{:S(2)}) async-start(bf16[4,16,2048]{2,1,0:T(8,128)(2,1)} %signed_pieces.1), calls=%async_computation | async-start | bytes 524288 | tf_op jit(solution)/shard_map/all_to_all | solution.py:345
  29.3 6.4 %collective-permute-start.1 = (bf16[64,2048]{1,0:T(8,128)(2,1)S(1)}, bf16[64,2048]{1,0:T(8,128)(2,1)S(1)}, u32[]{:S(2)}, u32[]{:S(2)}) collective-permute-start(bf16[64,2048]{1,0:T(8,128)(2,1)S(1)} %bitcast.2), channel_id=1, source_target_pairs={{0,8},{4,12},{8,0},{12,4},{16,24},{20,28},{24,16},{28,20},{1,9},{5... | collective-permute-start | bytes 786440 | tf_op jit(solution)/shard_map/ppermute | solution.py:27
  30.7 6.4 %collective-permute-start.2 = (bf16[64,2048]{1,0:T(8,128)(2,1)S(1)}, bf16[64,2048]{1,0:T(8,128)(2,1)S(1)}, u32[]{:S(2)}, u32[]{:S(2)}) collective-permute-start(bf16[64,2048]{1,0:T(8,128)(2,1)S(1)} %bitcast.3), channel_id=1, source_target_pairs={{0,16},{4,20},{8,24},{12,28},{16,0},{20,4},{24,8},{28,12},{1,17},{... | collective-permute-start | bytes 786440 | tf_op jit(solution)/shard_map/ppermute | solution.py:27
  32.3 21.1 %collective-permute-start.7 = (bf16[128,3584]{1,0:T(8,128)(2,1)S(1)}, bf16[128,3584]{1,0:T(8,128)(2,1)S(1)}, u32[]{:S(2)}, u32[]{:S(2)}) collective-permute-start(bf16[128,3584]{1,0:T(8,128)(2,1)S(1)} %copy-done), channel_id=1, source_target_pairs={{0,1},{1,0},{2,3},{3,2},{4,5},{5,4},{6,7},{7,6},{8,9},{9,8},{10,11... | collective-permute-start | bytes 2752520 | tf_op jit(solution)/shard_map/ppermute | solution.py:27
  32.5 20.9 %collective-permute-start.8 = (bf16[128,3584]{1,0:T(8,128)(2,1)S(1)}, bf16[128,3584]{1,0:T(8,128)(2,1)S(1)}, u32[]{:S(2)}, u32[]{:S(2)}) collective-permute-start(bf16[128,3584]{1,0:T(8,128)(2,1)S(1)} %copy-done), channel_id=1, source_target_pairs={{1,2},{2,1},{5,6},{6,5},{9,10},{10,9},{13,14},{14,13},{17,18},{18,... | collective-permute-start | bytes 2752520 | tf_op jit(solution)/shard_map/ppermute | solution.py:329
  33.2 5.6 %collective-permute-start = (bf16[64,2048]{1,0:T(8,128)(2,1)S(1)}, bf16[64,2048]{1,0:T(8,128)(2,1)S(1)}, u32[]{:S(2)}, u32[]{:S(2)}) collective-permute-start(bf16[64,2048]{1,0:T(8,128)(2,1)S(1)} %bitcast.4), channel_id=1, source_target_pairs={{0,4},{4,0},{8,12},{12,8},{16,20},{20,16},{24,28},{28,24},{1,5},{5... | collective-permute-start | bytes 786440 | tf_op jit(solution)/shard_map/ppermute | solution.py:27
  37.1 6.4 %collective-permute-start.5 = (bf16[64,2048]{1,0:T(8,128)(2,1)S(1)}, bf16[64,2048]{1,0:T(8,128)(2,1)S(1)}, u32[]{:S(2)}, u32[]{:S(2)}) collective-permute-start(bf16[64,2048]{1,0:T(8,128)(2,1)S(1)} %broadcast_select_fusion), channel_id=1, source_target_pairs={{0,16},{4,12},{8,24},{12,4},{16,0},{20,28},{24,8},{28,20},{1,17},{... | collective-permute-start | bytes 786440 | tf_op jit(solution)/shard_map/ppermute | solution.py:145
  38.7 4.8 %collective-permute-start.3 = (bf16[64,2048]{1,0:T(8,128)(2,1)S(1)}, bf16[64,2048]{1,0:T(8,128)(2,1)S(1)}, u32[]{:S(2)}, u32[]{:S(2)}) collective-permute-start(bf16[64,2048]{1,0:T(8,128)(2,1)S(1)} %collective-permute-done.1.refs_2_), channel_id=1, source_target_pairs={{0,4},{4,0},{8,12},{12,8},{16,20},{20,16},{24,28},{28,24},{1,5},{5... | collective-permute-start | bytes 786440 | tf_op jit(solution)/shard_map/ppermute | solution.py:27
  38.8 4.8 %collective-permute-start.4 = (bf16[64,2048]{1,0:T(8,128)(2,1)S(1)}, bf16[64,2048]{1,0:T(8,128)(2,1)S(1)}, u32[]{:S(2)}, u32[]{:S(2)}) collective-permute-start(bf16[64,2048]{1,0:T(8,128)(2,1)S(1)} %collective-permute-done.2.refs_4_), channel_id=1, source_target_pairs={{0,4},{4,0},{8,12},{12,8},{16,20},{20,16},{24,28},{28,24},{1,5},{5... | collective-permute-start | bytes 786440 | tf_op jit(solution)/shard_map/ppermute | solution.py:27
  43.6 1.5 %collective-permute-start.6 = (bf16[64,2048]{1,0:T(8,128)(2,1)S(1)}, bf16[64,2048]{1,0:T(8,128)(2,1)S(1)}, u32[]{:S(2)}, u32[]{:S(2)}) collective-permute-start(bf16[64,2048]{1,0:T(8,128)(2,1)S(1)} %collective-permute-done.5.refs_6_), channel_id=1, source_target_pairs={{0,4},{4,0},{8,12},{12,8},{16,20},{20,16},{24,28},{28,24},{1,5},{5... | collective-permute-start | bytes 786440 | tf_op jit(solution)/shard_map/ppermute | solution.py:27
  51.2 19.2 %collective-permute-start.9 = (bf16[256,1536]{1,0:T(8,128)(2,1)S(1)}, bf16[256,1536]{1,0:T(8,128)(2,1)S(1)}, u32[]{:S(2)}, u32[]{:S(2)}) collective-permute-start(bf16[256,1536]{1,0:T(8,128)(2,1)S(1)} %get-tuple-element.34), channel_id=1, source_target_pairs={{0,1},{3,2},{4,5},{7,6},{8,9},{11,10},{12,13},{15,14},{16,17},{19,... | collective-permute-start | bytes 2359304 | tf_op jit(solution)/shard_map/ppermute | solution.py:329
  53.4 21.5 %collective-permute-start.12 = (bf16[128,3584]{1,0:T(8,128)(2,1)S(1)}, bf16[128,3584]{1,0:T(8,128)(2,1)S(1)}, u32[]{:S(2)}, u32[]{:S(2)}) collective-permute-start(bf16[128,3584]{1,0:T(8,128)(2,1)S(1)} %collective-permute-done.7.e1), channel_id=1, source_target_pairs={{1,2},{2,1},{5,6},{6,5},{9,10},{10,9},{13,14},{14,13},{17,18},{18,... | collective-permute-start | bytes 2752520 | tf_op jit(solution)/shard_map/ppermute | solution.py:329
  54.1 24.3 %collective-permute-start.13 = (bf16[128,3584]{1,0:T(8,128)(2,1)S(1)}, bf16[128,3584]{1,0:T(8,128)(2,1)S(1)}, u32[]{:S(2)}, u32[]{:S(2)}) collective-permute-start(bf16[128,3584]{1,0:T(8,128)(2,1)S(1)} %collective-permute-done.8.o1), channel_id=1, source_target_pairs={{1,0},{2,3},{5,4},{6,7},{9,8},{10,11},{13,12},{14,15},{17,16},{18,... | collective-permute-start | bytes 2752520 | tf_op jit(solution)/shard_map/ppermute | solution.py:329
  70.4 26.3 %collective-permute-start.10 = (bf16[256,2048]{1,0:T(8,128)(2,1)S(1)}, bf16[256,2048]{1,0:T(8,128)(2,1)S(1)}, u32[]{:S(2)}, u32[]{:S(2)}) collective-permute-start(bf16[256,2048]{1,0:T(8,128)(2,1)S(1)} %get-tuple-element.35), channel_id=1, source_target_pairs={{0,1},{3,2},{4,5},{7,6},{8,9},{11,10},{12,13},{15,14},{16,17},{19,... | collective-permute-start | bytes 3145736 | tf_op jit(solution)/shard_map/ppermute | solution.py:329
  78.4 20.7 %collective-permute-start.15 = (bf16[128,3584]{1,0:T(8,128)(2,1)S(1)}, bf16[128,3584]{1,0:T(8,128)(2,1)S(1)}, u32[]{:S(2)}, u32[]{:S(2)}) collective-permute-start(bf16[128,3584]{1,0:T(8,128)(2,1)S(1)} %collective-permute-done.12.o2), channel_id=1, source_target_pairs={{1,0},{2,3},{5,4},{6,7},{9,8},{10,11},{13,12},{14,15},{17,16},{18,... | collective-permute-start | bytes 2752520 | tf_op jit(solution)/shard_map/ppermute | solution.py:329
  79.8 17.9 %collective-permute-start.14 = (bf16[256,1536]{1,0:T(8,128)(2,1)S(1)}, bf16[256,1536]{1,0:T(8,128)(2,1)S(1)}, u32[]{:S(2)}, u32[]{:S(2)}) collective-permute-start(bf16[256,1536]{1,0:T(8,128)(2,1)S(1)} %add_convert_fusion), channel_id=1, source_target_pairs={{1,2},{2,1},{5,6},{6,5},{9,10},{10,9},{13,14},{14,13},{17,18},{18,... | collective-permute-start | bytes 2359304 | tf_op jit(solution)/shard_map/ppermute | solution.py:329
  97.0 13.7 %collective-permute-start.11 = (bf16[128,2048]{1,0:T(8,128)(2,1)S(1)}, bf16[128,2048]{1,0:T(8,128)(2,1)S(1)}, u32[]{:S(2)}, u32[]{:S(2)}) collective-permute-start(bf16[128,2048]{1,0:T(8,128)(2,1)S(1)} %get-tuple-element.52), channel_id=1, source_target_pairs={{1,2},{2,1},{5,6},{6,5},{9,10},{10,9},{13,14},{14,13},{17,18},{18,... | collective-permute-start | bytes 1572872 | tf_op jit(solution)/shard_map/ppermute | solution.py:329
  99.2 11.5 %collective-permute-start.16 = (bf16[128,1536]{1,0:T(8,128)(2,1)S(1)}, bf16[128,1536]{1,0:T(8,128)(2,1)S(1)}, u32[]{:S(2)}, u32[]{:S(2)}) collective-permute-start(bf16[128,1536]{1,0:T(8,128)(2,1)S(1)} %add_convert_fusion.6), channel_id=1, source_target_pairs={{0,1},{1,0},{2,3},{3,2},{4,5},{5,4},{6,7},{7,6},{8,9},{9,8},{10,11... | collective-permute-start | bytes 1179656 | tf_op jit(solution)/shard_map/ppermute | solution.py:27
  103.2 21.5 %collective-permute-start.18 = (bf16[128,2048]{1,0:T(8,128)(2,1)S(1)}, bf16[128,2048]{1,0:T(8,128)(2,1)S(1)}, u32[]{:S(2)}, u32[]{:S(2)}) collective-permute-start(bf16[128,2048]{1,0:T(8,128)(2,1)S(1)} %get-tuple-element.53), channel_id=1, source_target_pairs={{1,2},{2,1},{5,6},{6,5},{9,10},{10,9},{13,14},{14,13},{17,18},{18,... | collective-permute-start | bytes 1572872 | tf_op jit(solution)/shard_map/ppermute | solution.py:329
  110.8 13.9 %collective-permute-start.17 = (bf16[128,2048]{1,0:T(8,128)(2,1)S(1)}, bf16[128,2048]{1,0:T(8,128)(2,1)S(1)}, u32[]{:S(2)}, u32[]{:S(2)}) collective-permute-start(bf16[128,2048]{1,0:T(8,128)(2,1)S(1)} %add_convert_fusion.3), channel_id=1, source_target_pairs={{0,1},{1,0},{2,3},{3,2},{4,5},{5,4},{6,7},{7,6},{8,9},{9,8},{10,11... | collective-permute-start | bytes 1572872 | tf_op jit(solution)/shard_map/ppermute | solution.py:27
